TPU v7x, 32 devices: a whole 2x2x4 slice. The times are simulated.
32 devices in a mesh: dp: 8 (over y, x, core), tensor: 4 (over z).
Axes of the slice: x: 2, y: 2, z: 4, core: 2. Of those that a mesh axis runs over, the one named last changes fastest.
Arguments:
- frames: float32 [8000, 768], P('dp'), may hold values from -6 to 6
- cotangent: float32 [8000, 768], P('dp'), may hold values from -6 to 6
- w_attn: float32 [2, 4, 768, 768], P(None, None, None, 'tensor'), may hold values from -4 to 4, as said below
- w_mlp: float32 [2, 2, 768, 3072], P(None, None, None, 'tensor'), may hold values from -4 to 4, as said below
- vectors: float32 [2, 6, 768], replicated, may hold values from -2 to 2, as said below
- head_bias: float32 [2, 2, 12, 64], P(None, None, 'tensor'), may hold values from -4 to 4
- up_bias: float32 [2, 48, 64], P(None, 'tensor'), may hold values from -4 to 4
- moment_attn: float32 [2, 4, 768, 768], P(None, None, 'dp', 'tensor')
- square_attn: float32 [2, 4, 768, 768], P(None, None, 'dp', 'tensor'), as said below
- moment_mlp: float32 [2, 2, 768, 3072], P(None, None, 'dp', 'tensor')
- square_mlp: float32 [2, 2, 768, 3072], P(None, None, 'dp', 'tensor'), as said below
- moment_vectors: float32 [2, 6, 768], P(None, None, 'dp')
- square_vectors: float32 [2, 6, 768], P(None, None, 'dp'), as said below
- moment_head: float32 [2, 2, 12, 64], P(None, None, 'tensor', 'dp')
- square_head: float32 [2, 2, 12, 64], P(None, None, 'tensor', 'dp'), as said below
- moment_up: float32 [2, 48, 64], P(None, 'tensor', 'dp')
- square_up: float32 [2, 48, 64], P(None, 'tensor', 'dp'), as said below
Outputs:
- layer_outputs: float32 [2, 8000, 768], P(None, 'dp')
- input_grad: float32 [8000, 768], P('dp')
- attn_new: float32 [2, 4, 768, 768], P(None, None, 'dp', 'tensor')
- attn_first: float32 [2, 4, 768, 768], P(None, None, 'dp', 'tensor')
- attn_second: float32 [2, 4, 768, 768], P(None, None, 'dp', 'tensor')
- mlp_new: float32 [2, 2, 768, 3072], P(None, None, 'dp', 'tensor')
- mlp_first: float32 [2, 2, 768, 3072], P(None, None, 'dp', 'tensor')
- mlp_second: float32 [2, 2, 768, 3072], P(None, None, 'dp', 'tensor')
- vectors_new: float32 [2, 6, 768], P(None, None, 'dp')
- vectors_first: float32 [2, 6, 768], P(None, None, 'dp')
- vectors_second: float32 [2, 6, 768], P(None, None, 'dp')
- head_new: float32 [2, 2, 12, 64], P(None, None, 'tensor', 'dp')
- head_first: float32 [2, 2, 12, 64], P(None, None, 'tensor', 'dp')
- head_second: float32 [2, 2, 12, 64], P(None, None, 'tensor', 'dp')
- up_new: float32 [2, 48, 64], P(None, 'tensor', 'dp')
- up_first: float32 [2, 48, 64], P(None, 'tensor', 'dp')
- up_second: float32 [2, 48, 64], P(None, 'tensor', 'dp')
Inputs may be any that keep to these rules, and one draw needn't show every extreme that they name: `w_attn`: independent entries. `w_mlp`: independent entries. `vectors`: gains near one, shifts and biases near zero. `square_attn`: positive. `square_mlp`: positive. `square_vectors`: positive. `square_head`: positive. `square_up`: positive.
All inputs are finite; a program needn't handle non-finite values.
Results may differ from a plain program's by a relative error of at most 0.019.
The roundings to bfloat16 on the way count: a program that leaves them out, or rounds other values in their place, can miss the bound.
Values sent between devices are 32-bit elements; how exact they have to be, the bound alone decides.
A program may use at most 192 MiB of HBM per device.

v0:
```python
import math

import jax
import jax.numpy as jnp
from jax import lax
from jax.sharding import PartitionSpec as P

HEAD_DIM = 64
FRAMES = 500
LAYERS = 2
STEP = 10


ln_eps = 1e-05
beta_one = 0.9
beta_two = 0.999
adam_eps = 1e-08
decay_rate = 0.01
rate_matrix = 0.05
rate_vector = 0.2


def product(left, right):
    return jnp.dot(left, right, preferred_element_type=jnp.float32)


def contract_last(left, right):
    return lax.dot_general(
        left, right, (((1,), (1,)), ((), ())), preferred_element_type=jnp.float32
    )


def contract_rows(left, right):
    return lax.dot_general(
        left, right, (((0,), (0,)), ((), ())), preferred_element_type=jnp.float32
    )


def normalize_kept(inputs, gain, shift):
    centre = jnp.mean(inputs, axis=-1, keepdims=True)
    centred = inputs - centre
    inverse = lax.rsqrt(jnp.mean(centred * centred, axis=-1, keepdims=True) + ln_eps)
    scaled = centred * inverse
    return (scaled * gain + shift, scaled, inverse)


def normalize_back(upstream, scaled, inverse, gain):
    gain_grad = jnp.sum(upstream * scaled, axis=0)
    shift_grad = jnp.sum(upstream, axis=0)
    inner_grad = upstream * gain
    lowered = inverse * (
        inner_grad
        - jnp.mean(inner_grad, axis=-1, keepdims=True)
        - scaled * jnp.mean(inner_grad * scaled, axis=-1, keepdims=True)
    )
    return (lowered, gain_grad, shift_grad)


def gelu_slope(before):
    return 0.5 * (1.0 + lax.erf(before * (1.0 / math.sqrt(2.0)))) + before * jnp.exp(
        -0.5 * before * before
    ) * (1.0 / math.sqrt(2.0 * math.pi))


def adamw_update(param, gradient, first, second, rate):
    first_new = beta_one * first + (1.0 - beta_one) * gradient
    second_new = beta_two * second + (1.0 - beta_two) * gradient * gradient
    ratio = (
        first_new
        / (1.0 - beta_one**STEP)
        / (jnp.sqrt(second_new / (1.0 - beta_two**STEP)) + adam_eps)
    )
    return (param - rate * (ratio + decay_rate * param), first_new, second_new)


def per_device(
    frames,
    cotangent,
    w_attn,
    w_mlp,
    vectors,
    head_bias,
    up_bias,
    moment_attn,
    square_attn,
    moment_mlp,
    square_mlp,
    moment_vectors,
    square_vectors,
    moment_head,
    square_head,
    moment_up,
    square_up,
):
    row_count = frames.shape[0]
    clip_count = row_count // FRAMES
    local_width = w_attn.shape[3]
    local_hidden = w_mlp.shape[3]
    local_heads = local_width // HEAD_DIM
    score_scale = 1.0 / math.sqrt(HEAD_DIM)

    def split_heads(block):
        return block.reshape(clip_count, FRAMES, local_heads, HEAD_DIM)

    def score_block(queries, keys_all):
        return (
            jnp.einsum("cqhd,ckhd->chqk", queries, keys_all, preferred_element_type=jnp.float32)
            * score_scale
        )

    hidden = frames
    stored = []
    sections = []
    for layer_index in range(LAYERS):
        row_params = vectors[layer_index]
        attn_low = w_attn[layer_index].astype(jnp.bfloat16)
        mlp_low = w_mlp[layer_index].astype(jnp.bfloat16)
        normed, scaled_one, inverse_one = normalize_kept(hidden, row_params[0], row_params[1])
        normed = normed.astype(jnp.bfloat16)
        queries = (
            product(normed, attn_low[0]) + head_bias[layer_index, 0].reshape(local_width)
        ).astype(jnp.bfloat16)
        keys_all = product(normed, attn_low[1]).astype(jnp.bfloat16)
        values_all = (
            product(normed, attn_low[2]) + head_bias[layer_index, 1].reshape(local_width)
        ).astype(jnp.bfloat16)
        scores = score_block(split_heads(queries), split_heads(keys_all))
        largest = jnp.max(scores, axis=-1, keepdims=True)
        logsum = largest + jnp.log(jnp.sum(jnp.exp(scores - largest), axis=-1, keepdims=True))
        probabilities = jnp.exp(scores - logsum).astype(jnp.bfloat16)
        mixture = jnp.einsum(
            "chqk,ckhd->cqhd",
            probabilities,
            split_heads(values_all),
            preferred_element_type=jnp.float32,
        )
        mixture = mixture.reshape(row_count, local_width).astype(jnp.bfloat16)
        branch = lax.psum(contract_last(mixture, attn_low[3]), "tensor") + row_params[4]
        middle = hidden + branch
        normed_two, scaled_two, inverse_two = normalize_kept(middle, row_params[2], row_params[3])
        normed_two = normed_two.astype(jnp.bfloat16)
        before = product(normed_two, mlp_low[0]) + up_bias[layer_index].reshape(local_hidden)
        activated = jax.nn.gelu(before, approximate=False).astype(jnp.bfloat16)
        hidden = middle + (lax.psum(contract_last(activated, mlp_low[1]), "tensor") + row_params[5])
        sections.append(hidden)
        stored.append(
            (
                attn_low,
                mlp_low,
                normed,
                scaled_one,
                inverse_one,
                queries,
                keys_all,
                values_all,
                logsum,
                mixture,
                normed_two,
                scaled_two,
                inverse_two,
                before,
                activated,
            )
        )
    upstream = cotangent
    grad_layers = [None] * LAYERS
    for layer_index in reversed(range(LAYERS)):
        (
            attn_low,
            mlp_low,
            normed,
            scaled_one,
            inverse_one,
            queries,
            keys_all,
            values_all,
            logsum,
            mixture,
            normed_two,
            scaled_two,
            inverse_two,
            before,
            activated,
        ) = stored[layer_index]
        row_params = vectors[layer_index]
        output_low = upstream.astype(jnp.bfloat16)
        down_bias_grad = jnp.sum(output_low.astype(jnp.float32), axis=0)
        down_grad = contract_rows(output_low, activated)
        before_back = (product(output_low, mlp_low[1]) * gelu_slope(before)).astype(jnp.bfloat16)
        up_bias_grad = jnp.sum(before_back.astype(jnp.float32), axis=0)
        up_grad = contract_rows(normed_two, before_back)
        normed_two_grad = lax.psum(contract_last(before_back, mlp_low[0]), "tensor")
        lowered, gain_two_grad, shift_two_grad = normalize_back(
            normed_two_grad, scaled_two, inverse_two, row_params[2]
        )
        upstream = upstream + lowered
        branch_low = upstream.astype(jnp.bfloat16)
        out_bias_grad = jnp.sum(branch_low.astype(jnp.float32), axis=0)
        out_grad = contract_rows(branch_low, mixture)
        mixture_back = split_heads(product(branch_low, attn_low[3]).astype(jnp.bfloat16))
        query_heads = split_heads(queries)
        key_heads = split_heads(keys_all)
        probabilities = jnp.exp(score_block(query_heads, key_heads) - logsum)
        prob_grad = jnp.einsum(
            "cqhd,ckhd->chqk",
            mixture_back,
            split_heads(values_all),
            preferred_element_type=jnp.float32,
        )
        centre = jnp.sum(prob_grad * probabilities, axis=-1, keepdims=True)
        score_back = (probabilities * (prob_grad - centre)).astype(jnp.bfloat16)
        query_back = (
            (
                jnp.einsum(
                    "chqk,ckhd->cqhd", score_back, key_heads, preferred_element_type=jnp.float32
                )
                * score_scale
            )
            .astype(jnp.bfloat16)
            .reshape(row_count, local_width)
        )
        key_back = (
            (
                jnp.einsum(
                    "chqk,cqhd->ckhd", score_back, query_heads, preferred_element_type=jnp.float32
                )
                * score_scale
            )
            .astype(jnp.bfloat16)
            .reshape(row_count, local_width)
        )
        value_back = (
            jnp.einsum(
                "chqk,cqhd->ckhd",
                probabilities.astype(jnp.bfloat16),
                mixture_back,
                preferred_element_type=jnp.float32,
            )
            .astype(jnp.bfloat16)
            .reshape(row_count, local_width)
        )
        query_weight_grad = contract_rows(normed, query_back)
        key_weight_grad = contract_rows(normed, key_back)
        value_weight_grad = contract_rows(normed, value_back)
        normed_partial = (
            contract_last(query_back, attn_low[0])
            + contract_last(key_back, attn_low[1])
            + contract_last(value_back, attn_low[2])
        )
        normed_grad = lax.psum(normed_partial, "tensor")
        lowered, gain_one_grad, shift_one_grad = normalize_back(
            normed_grad, scaled_one, inverse_one, row_params[0]
        )
        upstream = upstream + lowered
        attn_grad = jnp.stack([query_weight_grad, key_weight_grad, value_weight_grad, out_grad])
        mlp_grad = jnp.stack([up_grad, down_grad])
        vector_grad = jnp.stack(
            [
                gain_one_grad,
                shift_one_grad,
                gain_two_grad,
                shift_two_grad,
                out_bias_grad,
                down_bias_grad,
            ]
        )
        head_grad = jnp.stack(
            [
                jnp.sum(query_back.astype(jnp.float32), axis=0),
                jnp.sum(value_back.astype(jnp.float32), axis=0),
            ]
        ).reshape(2, local_heads, HEAD_DIM)
        up_grad_rows = up_bias_grad.reshape(local_hidden // HEAD_DIM, HEAD_DIM)
        grad_layers[layer_index] = (attn_grad, mlp_grad, vector_grad, head_grad, up_grad_rows)
    stacked = [
        jnp.stack([grad_layers[layer_index][member] for layer_index in range(LAYERS)])
        for member in range(5)
    ]
    summed = (
        lax.psum_scatter(stacked[0], "dp", scatter_dimension=2, tiled=True),
        lax.psum_scatter(stacked[1], "dp", scatter_dimension=2, tiled=True),
        lax.psum_scatter(stacked[2], "dp", scatter_dimension=2, tiled=True),
        lax.psum_scatter(stacked[3], "dp", scatter_dimension=3, tiled=True),
        lax.psum_scatter(stacked[4], "dp", scatter_dimension=2, tiled=True),
    )
    owner_index = lax.axis_index("dp")
    owner_count = lax.axis_size("dp")

    def owned(param, dim):
        piece_size = param.shape[dim] // owner_count
        return lax.dynamic_slice_in_dim(param, owner_index * piece_size, piece_size, dim)

    attn = adamw_update(owned(w_attn, 2), summed[0], moment_attn, square_attn, rate_matrix)
    mlp = adamw_update(owned(w_mlp, 2), summed[1], moment_mlp, square_mlp, rate_matrix)
    vector_new = adamw_update(
        owned(vectors, 2), summed[2], moment_vectors, square_vectors, rate_vector
    )
    head = adamw_update(owned(head_bias, 3), summed[3], moment_head, square_head, rate_vector)
    upper = adamw_update(owned(up_bias, 2), summed[4], moment_up, square_up, rate_vector)
    return (
        jnp.stack(sections),
        upstream,
        attn[0],
        attn[1],
        attn[2],
        mlp[0],
        mlp[1],
        mlp[2],
        vector_new[0],
        vector_new[1],
        vector_new[2],
        head[0],
        head[1],
        head[2],
        upper[0],
        upper[1],
        upper[2],
    )


def solution(mesh):
    in_specs = (
        P("dp", None),
        P("dp", None),
        P(None, None, None, "tensor"),
        P(None, None, None, "tensor"),
        P(),
        P(None, None, "tensor", None),
        P(None, "tensor", None),
        P(None, None, "dp", "tensor"),
        P(None, None, "dp", "tensor"),
        P(None, None, "dp", "tensor"),
        P(None, None, "dp", "tensor"),
        P(None, None, "dp"),
        P(None, None, "dp"),
        P(None, None, "tensor", "dp"),
        P(None, None, "tensor", "dp"),
        P(None, "tensor", "dp"),
        P(None, "tensor", "dp"),
    )
    out_specs = (
        P(None, "dp", None),
        P("dp", None),
        P(None, None, "dp", "tensor"),
        P(None, None, "dp", "tensor"),
        P(None, None, "dp", "tensor"),
        P(None, None, "dp", "tensor"),
        P(None, None, "dp", "tensor"),
        P(None, None, "dp", "tensor"),
        P(None, None, "dp"),
        P(None, None, "dp"),
        P(None, None, "dp"),
        P(None, None, "tensor", "dp"),
        P(None, None, "tensor", "dp"),
        P(None, None, "tensor", "dp"),
        P(None, "tensor", "dp"),
        P(None, "tensor", "dp"),
        P(None, "tensor", "dp"),
    )
    return jax.shard_map(
        per_device, mesh=mesh, in_specs=in_specs, out_specs=out_specs, check_vma=False
    )
```

profile of v0, /device:TPU:0, one launch (start us, length us, event | category | flops | bytes accessed | tf_op | source)
XLA Modules:
  0.0 1338.9 jit_solution(3130817452486266947)
XLA Ops:
  44.1 6.3 convert.9
  50.5 114.8 %all-reduce.12.cloned.1.call-done = f32[1000,768]{1,0:T(8,128)} async-done(((f32[1000,768]{1,0:T(8,128)}), f32[1000,768]{1,0:T(8,128)}) %all-reduce.12.cloned.1.call-update) | async-done | bytes 3072016 | tf_op jit(solution)/shard_map/psum | solution.py:138
  168.6 9.1 fusion.4
  181.5 117.2 %all-reduce.14.cloned.1.call-done = f32[1000,768]{1,0:T(8,128)} async-done(((f32[1000,768]{1,0:T(8,128)}), f32[1000,768]{1,0:T(8,128)}) %all-reduce.14.cloned.1.call-update) | async-done | bytes 3072016 | tf_op jit(solution)/shard_map/psum | solution.py:144
  328.5 117.7 %all-reduce.16.cloned.1.call-done = f32[1000,768]{1,0:T(8,128)} async-done(((f32[1000,768]{1,0:T(8,128)}), f32[1000,768]{1,0:T(8,128)}) %all-reduce.16.cloned.1.call-update) | async-done | bytes 3072016 | tf_op jit(solution)/shard_map/psum | solution.py:138
  449.4 8.7 fusion.7
  466.1 117.5 %all-reduce.18.cloned.1.call-done = f32[1000,768]{1,0:T(8,128)} async-done(((f32[1000,768]{1,0:T(8,128)}), f32[1000,768]{1,0:T(8,128)}) %all-reduce.18.cloned.1.call-update) | async-done | bytes 3072016 | tf_op jit(solution)/shard_map/psum | solution.py:192
  588.2 4.1 convert_reduce_fusion.3
  597.8 5.4 convert_reduce_fusion.6
  603.2 4.7 multiply_reduce_fusion.1
  632.5 117.7 %all-reduce.20.cloned.1.call-done = f32[1000,768]{1,0:T(8,128)} async-done(((f32[1000,768]{1,0:T(8,128)}), f32[1000,768]{1,0:T(8,128)}) %all-reduce.20.cloned.1.call-update) | async-done | bytes 3072016 | tf_op jit(solution)/shard_map/psum | solution.py:250
  763.9 4.7 fusion.56
  768.6 113.2 %all-reduce.22.cloned.1.call-done = f32[1000,768]{1,0:T(8,128)} async-done(((f32[1000,768]{1,0:T(8,128)}), f32[1000,768]{1,0:T(8,128)}) %all-reduce.22.cloned.1.call-update) | async-done | bytes 3072016 | tf_op jit(solution)/shard_map/psum | solution.py:192
  881.8 4.5 multiply_reduce_fusion.6
  895.2 5.5 convert_reduce_fusion.8
  900.8 4.7 multiply_reduce_fusion
  948.9 200.4 %all-reduce.24.cloned.1.call-done = (f32[1000,768]{1,0:T(8,128)}, f32[1000,768]{1,0:T(8,128)}) async-done(((f32[1000,768]{1,0:T(8,128)}, f32[1000,768]{1,0:T(8,128)}), (f32[1000,768]{1,0:T(8,128)}, f32[1000,768]{1,0:T(8,128)})) %all-reduce.24.cloned.1.call-update) | async-done | bytes 6144016 | tf_op jit(solution)/shard_map/psum | solution.py:144
  1156.5 4.9 pad_maximum_fusion.2
  1161.4 7.3 copy.242
  1168.7 8.3 reshape.276
  1190.4 4.2 pad_maximum_fusion
  1202.6 26.0 %all-reduce.2 = (f32[2,2,3,64]{3,2,1,0:T(4,128)S(1)}, f32[2,12,64]{1,0,2:T(2,128)S(1)}) all-reduce(f32[2,2,3,64]{3,2,1,0:T(4,128)S(1)} %maximum_maximum_fusion, f32[2,12,64]{1,0,2:T(2,128)S(1)} %copy.220), channel_id=5, replica_groups=mesh['dp'=8,'tensor'=4] {'dp'}, use_global_device_ids=true, to_apply=%region_49.0.clone | all-reduce | flops 2304 | bytes 18432
  1259.8 67.8 %reduce-scatter.9.cloned.1.call-done = f32[2,2,96,768]{3,2,1,0:T(8,128)} async-done(((f32[2,2,768,768]{3,2,1,0:T(8,128)}), f32[2,2,96,768]{3,2,1,0:T(8,128)}) %reduce-scatter.9.cloned.1.call-update) | async-done | bytes 1179664 | tf_op jit(solution)/shard_map/reduce_scatter | solution.py:281
  1327.6 4.3 multiply_subtract_fusion
  (410 shorter events, 243.2 us)
Async XLA Ops:
  7.2 158.2 %all-reduce.12.cloned.1.call-start = ((), (), s32[]{:S(2)}) async-start(), calls=%async_computation.3 | async-start | bytes 6144000 | tf_op jit(solution)/shard_map/psum | solution.py:138
  8.9 159.4 %copy-start.87 = (f32[768]{0:T(1024)}, f32[768]{0:T(1024)S(1)}, u32[]{:S(2)}) copy-start(f32[768]{0:T(1024)S(1)} %get-tuple-element.108) | copy-start | bytes 9220
  8.9 440.2 %copy-start.89 = (f32[768]{0:T(1024)}, f32[768]{0:T(1024)S(1)}, u32[]{:S(2)}) copy-start(f32[768]{0:T(1024)S(1)} %get-tuple-element.102) | copy-start | bytes 9220
  43.8 254.9 %all-reduce.14.cloned.1.call-start = ((), (), s32[]{:S(2)}) async-start(), calls=%async_computation.4 | async-start | bytes 6144000 | tf_op jit(solution)/shard_map/psum | solution.py:144
  50.5 117.8 %copy-start.85 = (f32[768]{0:T(1024)}, f32[768]{0:T(1024)S(1)}, u32[]{:S(2)}) copy-start(f32[768]{0:T(1024)S(1)} %add.365) | copy-start | bytes 9220
  180.7 265.5 %all-reduce.16.cloned.1.call-start = ((), (), s32[]{:S(2)}) async-start(), calls=%async_computation.5 | async-start | bytes 6144000 | tf_op jit(solution)/shard_map/psum | solution.py:138
  328.2 255.4 %all-reduce.18.cloned.1.call-start = ((), (), s32[]{:S(2)}) async-start(), calls=%async_computation.6 | async-start | bytes 6144000 | tf_op jit(solution)/shard_map/psum | solution.py:192
  465.6 284.6 %all-reduce.20.cloned.1.call-start = ((), (), s32[]{:S(2)}) async-start(), calls=%async_computation.7 | async-start | bytes 6144000 | tf_op jit(solution)/shard_map/psum | solution.py:250
  597.8 10.1 slice-start.2
  632.3 249.5 %all-reduce.22.cloned.1.call-start = ((), (), s32[]{:S(2)}) async-start(), calls=%async_computation.8 | async-start | bytes 6144000 | tf_op jit(solution)/shard_map/psum | solution.py:192
  763.8 385.5 %all-reduce.24.cloned.1.call-start = ((), (), s32[]{:S(2)}) async-start(), calls=%async_computation.12 | async-start | bytes 12288000 | tf_op jit(solution)/shard_map/psum | solution.py:144
  895.2 10.2 slice-start
  931.6 311.2 %reduce-scatter.13.cloned.1.call-start = ((), (), s32[]{:S(2)}) async-start(), calls=%async_computation.11 | async-start | bytes 442368
  947.3 202.0 %copy-start.58 = (f32[1000]{0:T(1024)S(1)}, f32[1000]{0:T(1024)}, u32[]{:S(2)}) copy-start(f32[1000]{0:T(1024)} %copy-done.57) | copy-start | bytes 12004
  947.3 202.0 %copy-start.60 = (f32[1000]{0:T(1024)S(1)}, f32[1000]{0:T(1024)}, u32[]{:S(2)}) copy-start(f32[1000]{0:T(1024)} %copy-done.59) | copy-start | bytes 12004
  947.4 202.0 %copy-start.62 = (f32[768]{0:T(1024)S(1)}, f32[768]{0:T(1024)}, u32[]{:S(2)}) copy-start(f32[768]{0:T(1024)} %copy-done.61) | copy-start | bytes 9220
  1156.5 90.8 %reduce-scatter.11.cloned.1.call-start = ((), (), s32[]{:S(2)}) async-start(), calls=%async_computation.10 | async-start | bytes 5308416
  1177.1 150.5 %reduce-scatter.9.cloned.1.call-start = ((), (), s32[]{:S(2)}) async-start(), calls=%async_computation.9 | async-start | bytes 10616832 | tf_op jit(solution)/shard_map/reduce_scatter | solution.py:281
  1194.7 33.9 %copy-start.79 = (f32[2,2,3,8]{3,1,2,0:T(2,128)S(1)}, f32[2,2,3,8]{3,1,2,0:T(2,128)}, u32[]{:S(2)}) copy-start(f32[2,2,3,8]{3,1,2,0:T(2,128)} %param.30) | copy-start | bytes 1156
  1194.7 33.9 %copy-start.80 = (f32[2,2,3,8]{3,1,2,0:T(2,128)S(1)}, f32[2,2,3,8]{3,1,2,0:T(2,128)}, u32[]{:S(2)}) copy-start(f32[2,2,3,8]{3,1,2,0:T(2,128)} %param.31) | copy-start | bytes 1156
  1194.7 35.8 %copy-start.77 = (f32[2,12,8]{1,2,0:T(8,128)S(1)}, f32[2,12,8]{1,2,0:T(8,128)}, u32[]{:S(2)}) copy-start(f32[2,12,8]{1,2,0:T(8,128)} %param.32) | copy-start | bytes 2308
  1194.7 35.8 %copy-start.78 = (f32[2,12,8]{1,2,0:T(8,128)S(1)}, f32[2,12,8]{1,2,0:T(8,128)}, u32[]{:S(2)}) copy-start(f32[2,12,8]{1,2,0:T(8,128)} %param.33) | copy-start | bytes 2308
  1194.8 36.4 %copy-start.67 = (f32[768]{0:T(1024)S(1)}, f32[768]{0:T(1024)}, u32[]{:S(2)}) copy-start(f32[768]{0:T(1024)} %get-tuple-element.101) | copy-start | bytes 9220
  1253.7 73.9 %copy-start.54 = (f32[2,2,96,768]{3,2,1,0:T(8,128)S(1)}, f32[2,2,96,768]{3,2,1,0:T(8,128)}, u32[]{:S(2)}) copy-start(f32[2,2,96,768]{3,2,1,0:T(8,128)} %param.26) | copy-start | bytes 3538948
  (95 other events, 387.3 us)
Sparse Core Ops, SparseCore 0:
  43.9 121.4 all-reduce.11
  180.8 117.7 all-reduce.13
  328.3 117.8 all-reduce.15
  465.7 117.7 all-reduce.17
  632.4 117.7 all-reduce.19
  764.0 117.7 all-reduce.21
  931.7 217.6 all-reduce.23
  1156.6 32.7 reduce-scatter.12
  1192.9 54.3 reduce-scatter.10
  1251.1 76.4 reduce-scatter.8
where the time goes:
time: 1350 us; the launch traced here: 1340 us
  waiting for transfers between devices  968 us (72%)
  matrix products  142 us (11%)
  local copies, waits for them, and re-layouts  101 us (7%)
  other arithmetic  83 us (6%)
  blocking collectives  26 us (2%)
  between operations  16.6 us (1%)
    psum x2, waiting for transfers between devices, per_device(): lax.psum(contract_last(activated, mlp_low[1]), 'tensor') + row_params[5]  318 us
    psum x2, waiting for transfers between devices, per_device(): lax.psum(contract_last(mixture, attn_low[3]), 'tensor') + row_params[4]  233 us
    psum x2, waiting for transfers between devices, per_device(): normed_two_grad = lax.psum(contract_last(before_back, mlp_low[0]), 'tensor')  231 us
    psum x1, waiting for transfers between devices, per_device(): normed_grad = lax.psum(normed_partial, 'tensor')  118 us
    reduce_scatter x1, waiting for transfers between devices, per_device(): lax.psum_scatter(stacked[1], 'dp', scatter_dimension=2, tiled=True)  67.8 us
    unnamed x240, local copies, waits for them, and re-layouts  56.5 us
    dot_general x12, matrix products, product(): return jnp.dot(left, right, preferred_element_type=jnp.float32)  43.2 us
    dot_general x12, matrix products, contract_last(): lax.dot_general(left, right, (((1,), (1,)), ((), ())), preferred_element_...  37.8 us
  transfers between devices with their start and end apart: 10, of which 9 were waited for; matrix products, arithmetic and copies ran while one was open for 7% of the time, Pallas kernels for 0%

commit v1 on v0

v1 whole, which is shorter than its diff:
```python
import math
from types import SimpleNamespace

import jax
import jax.numpy as jnp
from jax import lax
from jax.experimental import pallas as pl
from jax.experimental.pallas import tpu as pltpu
from jax.sharding import PartitionSpec as P

HEAD_DIM = 64
FRAMES = 500
ROWS = 512
LAYERS = 2
STEP = 10
WIDTH = 768
BLOCK = 384
UNITS = 6
TOTAL = LAYERS * UNITS
GROUP = 8
HEADS_HERE = 3
SLOTS = 4

ln_eps = 1e-05
beta_one = 0.9
beta_two = 0.999
adam_eps = 1e-08
decay_rate = 0.01
rate_matrix = 0.05
rate_vector = 0.2
score_scale = 1.0 / math.sqrt(HEAD_DIM)
MESH = pl.DeviceIdType.MESH
f32 = jnp.float32
bf16 = jnp.bfloat16
ANY = pl.BlockSpec(memory_space=pl.ANY)
VMEM = pl.BlockSpec(memory_space=pltpu.VMEM)


def product(left, right):
    return jnp.dot(left, right, preferred_element_type=f32)


def contract_last(left, right):
    return lax.dot_general(left, right, (((1,), (1,)), ((), ())), preferred_element_type=f32)


def contract_rows(left, right):
    return lax.dot_general(left, right, (((0,), (0,)), ((), ())), preferred_element_type=f32)


def normalize_parts(inputs):
    centre = jnp.mean(inputs, axis=-1, keepdims=True)
    centred = inputs - centre
    inverse = lax.rsqrt(jnp.mean(centred * centred, axis=-1, keepdims=True) + ln_eps)
    return centred * inverse, inverse


def normalize_back(upstream, scaled, inverse, gain):
    gain_grad = jnp.sum(upstream * scaled, axis=0)
    shift_grad = jnp.sum(upstream, axis=0)
    inner_grad = upstream * gain
    lowered = inverse * (
        inner_grad
        - jnp.mean(inner_grad, axis=-1, keepdims=True)
        - scaled * jnp.mean(inner_grad * scaled, axis=-1, keepdims=True)
    )
    return (lowered, gain_grad, shift_grad)


def gelu(before):
    return 0.5 * before * (1.0 + lax.erf(before * (1.0 / math.sqrt(2.0))))


def gelu_slope(before):
    return 0.5 * (1.0 + lax.erf(before * (1.0 / math.sqrt(2.0)))) + before * jnp.exp(
        -0.5 * before * before
    ) * (1.0 / math.sqrt(2.0 * math.pi))


def adamw_update(param, gradient, first, second, rate):
    first_new = beta_one * first + (1.0 - beta_one) * gradient
    second_new = beta_two * second + (1.0 - beta_two) * gradient * gradient
    ratio = (
        first_new
        / (1.0 - beta_one**STEP)
        / (jnp.sqrt(second_new / (1.0 - beta_two**STEP)) + adam_eps)
    )
    return (param - rate * (ratio + decay_rate * param), first_new, second_new)


def find_place():
    dp = lax.axis_index("dp")
    t = lax.axis_index("tensor")
    i = lax.rem(dp, GROUP)
    base = dp - i
    c = lax.rem(i, 2)
    x = lax.rem(i // 2, 2)
    y = i // 4
    up = 1 - 2 * c
    level = c * (3 - t) + (1 - c) * t

    def at(cc, xx, yy):
        return base + 4 * yy + 2 * xx + cc

    return SimpleNamespace(
        t=t,
        c=c,
        x=x,
        y=y,
        q=2 * y + x,
        qx=2 * y + 1 - x,
        qy=2 * (1 - y) + x,
        qd=2 * (1 - y) + 1 - x,
        level=level,
        partner=(at(1 - c, x, y), t),
        xn=(at(c, 1 - x, y), t),
        yn=(at(c, x, 1 - y), t),
        above=(dp, t + up),
        below=(dp, t - up),
    )


def greet(p):
    barrier = pltpu.get_barrier_semaphore()

    def signal(device):
        pl.semaphore_signal(barrier, inc=1, device_id=device, device_id_type=MESH)

    signal(p.partner)
    signal(p.xn)
    signal(p.yn)

    @pl.when(p.level < 3)
    def _():
        signal(p.above)

    @pl.when(p.level > 0)
    def _():
        signal(p.below)

    inner = (p.level > 0) & (p.level < 3)

    @pl.when(inner)
    def _():
        pl.semaphore_wait(barrier, 5)

    @pl.when(jnp.logical_not(inner))
    def _():
        pl.semaphore_wait(barrier, 4)


def remote(src, dst, send_sem, recv_sem, device):
    return pltpu.make_async_remote_copy(
        src_ref=src,
        dst_ref=dst,
        send_sem=send_sem,
        recv_sem=recv_sem,
        device_id=device,
        device_id_type=MESH,
    )


def local(src, dst, sem):
    return pltpu.make_async_copy(src, dst, sem)


def forward_kernel(
    frames,
    cotangent,
    wa,
    wm,
    bias,
    vec,
    o_x,
    o_ct,
    o_h,
    o_m,
    o_n1,
    o_n2,
    o_q,
    o_k,
    o_v,
    o_a,
    o_u,
    o_c,
    o_w,
    gathered,
    biases,
    hs,
    ms,
    n1s,
    n2s,
    qs,
    ks,
    vs,
    as_,
    us,
    cs,
    low,
    part,
    other,
    rz,
    sz,
    szd,
    rx,
    sx,
    ry,
    sy,
    rxd,
    sxd,
    ryd,
    syd,
    native,
    first_sem,
    bias_sem,
    swap_sem,
    low_sem,
    mid_sem,
    out_sem,
):
    p = find_place()
    greet(p)
    level = p.level

    def when(cond):
        return pl.when(cond)

    mine = (p.t // 2) == p.c
    clip = lax.rem(p.t, 2)
    inputs = ((frames, hs.at[0], 0), (frames, o_x, 1), (cotangent, o_ct, 2))

    @when(mine)
    def _():
        for source, target, k in inputs:
            local(source.at[clip], target, first_sem.at[k]).start()
            remote(source.at[clip], target, first_sem.at[3 + k], first_sem.at[6 + k], p.partner).start()

    def wait_input(k):
        source, target, _ = inputs[k]

        @when(mine)
        def _():
            local(source.at[clip], target, first_sem.at[k]).wait()
            remote(source.at[clip], target, first_sem.at[3 + k], first_sem.at[6 + k], p.partner).wait_send()

        @when(jnp.logical_not(mine))
        def _():
            remote(source.at[clip], target, first_sem.at[3 + k], first_sem.at[6 + k], p.partner).wait_recv()

    def bias_copy(src, j, k, device):
        return remote(src, biases.at[j], bias_sem.at[k], bias_sem.at[3 + j], device)

    @when(level == 0)
    def _():
        local(bias, biases.at[0], bias_sem.at[5]).start()
        bias_copy(bias, 0, 0, p.above).start()

    @when(level == 1)
    def _():
        local(bias, biases.at[1], bias_sem.at[5]).start()
        bias_copy(bias, 1, 1, p.above).start()
        bias_copy(bias, 1, 2, p.below).start()

    def block(l, i, q=None):
        if i < 2:
            return wa.at[l, i] if q is None else wa.at[l, i, q]
        k, cols = (i - 2) // 2, pl.ds(BLOCK * ((i - 2) % 2), BLOCK)
        return wm.at[l, k, :, :, :, cols] if q is None else wm.at[l, k, q, :, :, cols]

    def z_copy(src, u, j, device, send_sem):
        return remote(src, gathered.at[j, u, p.q], send_sem, rz.at[u, j], device)

    def x_copy(u, j, q):
        return remote(gathered.at[j, u, q], gathered.at[j, u, q], sx.at[u, j], rx.at[u, j], p.xn)

    def y_copy(u, j, q):
        return remote(gathered.at[j, u, q], gathered.at[j, u, q], sy.at[u, j], ry.at[u, j], p.yn)

    def xd_copy(u, j, q):
        return remote(gathered.at[j, u, q, 1], gathered.at[j, u, q, 1], sxd.at[u, j], rxd.at[u, j], p.xn)

    def yd_copy(u, j, q):
        return remote(gathered.at[j, u, q, 0], gathered.at[j, u, q, 0], syd.at[u, j], ryd.at[u, j], p.yn)

    def source(l, i):
        u = UNITS * l + i

        @when(level == 0)
        def _():
            z_copy(block(l, i, p.q), u, 0, p.above, sz.at[u, 0]).start()
            local(block(l, i), gathered.at[0, u], native.at[u]).start()

        @when(level == 1)
        def _():
            z_copy(block(l, i, p.q), u, 1, p.above, sz.at[u, 1]).start()
            z_copy(block(l, i, p.q), u, 1, p.below, szd.at[u]).start()
            local(block(l, i), gathered.at[1, u], native.at[u]).start()

    def stage_one(l, i):
        u = UNITS * l + i
        for j in range(2):

            @when(level != j)
            def _(j=j):
                here = gathered.at[j, u, p.q]
                z_copy(here, u, j, p.above, sz.at[u, j]).wait_recv()

                @when((level == 2) | ((level == 1) if j == 0 else (level == 2)))
                def _():
                    z_copy(here, u, j, p.above, sz.at[u, j]).start()

                x_copy(u, j, p.q).start()
                y_copy(u, j, p.q).start()

    def stage_two(l, i):
        u = UNITS * l + i
        for j in range(2):

            @when(level != j)
            def _(j=j):
                x_copy(u, j, p.qx).wait_recv()
                yd_copy(u, j, p.qx).start()
                y_copy(u, j, p.qy).wait_recv()
                xd_copy(u, j, p.qy).start()

    def finish(l, i):
        u = UNITS * l + i
        for j in range(2):

            @when(level != j)
            def _(j=j):
                yd_copy(u, j, p.qd).wait_recv()
                xd_copy(u, j, p.qd).wait_recv()

            @when(level == j)
            def _(j=j):
                local(block(l, i), gathered.at[j, u], native.at[u]).wait()

    def ahead(step, l, i, by):
        k = i + by
        if k < UNITS:
            step(l, k)
        else:

            @when(l + k // UNITS < LAYERS)
            def _():
                step(l + k // UNITS, k % UNITS)

    def tick(l, i):
        ahead(source, l, i, 3)
        ahead(stage_one, l, i, 2)
        ahead(stage_two, l, i, 1)
        finish(l, i)

    for i in range(3):
        source(0, i)
    bias_wait = bias_copy(bias, 0, 0, p.above)

    @when(level != 0)
    def _():
        bias_wait.wait_recv()

    @when((level == 1) | (level == 2))
    def _():
        bias_copy(biases.at[0], 0, 0, p.above).start()

    @when(level != 1)
    def _():
        bias_copy(bias, 1, 1, p.above).wait_recv()

    @when(level == 2)
    def _():
        bias_copy(biases.at[1], 1, 1, p.above).start()

    @when(level < 2)
    def _():
        local(bias, biases.at[0], bias_sem.at[5]).wait()

    wait_input(0)
    stage_one(0, 0)
    stage_one(0, 1)
    stage_two(0, 0)

    def unit_low(u, j):
        value = gathered[j, u].reshape(WIDTH, BLOCK).astype(bf16)
        return value

    def keep_low(l, i):
        u = UNITS * l + i
        slot = i % 2

        def drain():
            for j in range(2):
                local(low.at[slot, j], o_w.at[j, u], low_sem.at[slot, j]).wait()

        if i >= 2:
            drain()
        else:
            pl.when(l > 0)(drain)
        for j in range(2):
            low[slot, j] = unit_low(u, j)
            local(low.at[slot, j], o_w.at[j, u], low_sem.at[slot, j]).start()
        return low.at[slot]

    def swap(slot):
        copy = remote(part, other.at[slot], swap_sem.at[slot], swap_sem.at[2 + slot], p.partner)
        copy.start()
        copy.wait()

    def out_copies(l):
        return [
            local(hs.at[l + 1], o_h.at[l], out_sem.at[0, l]),
            local(ms.at[l], o_m.at[l], out_sem.at[1, l]),
            local(n1s.at[l], o_n1.at[l], out_sem.at[2, l]),
            local(n2s.at[l], o_n2.at[l], out_sem.at[3, l]),
            local(qs.at[l], o_q.at[l], out_sem.at[4, l]),
            local(ks.at[l], o_k.at[l], out_sem.at[5, l]),
            local(vs.at[l], o_v.at[l], out_sem.at[6, l]),
            local(as_.at[l], o_a.at[l], out_sem.at[7, l]),
        ]

    def mid_copies(l, i):
        k = i - 2
        return [
            local(us.at[:, k], o_u.at[l, :, k], mid_sem.at[0, k]),
            local(cs.at[:, k], o_c.at[l, :, k], mid_sem.at[1, k]),
        ]

    def layer(l, carry):
        params = vec[l]

        tick(l, 0)
        scaled, _ = normalize_parts(hs[l])
        n1s[l] = (scaled * params[0:1] + params[1:2]).astype(bf16)
        weights = keep_low(l, 0)
        for j in range(2):
            both = product(n1s[l], weights[j])
            qs[l, j] = (both[:, :192] + biases[j, pl.ds(3 * l, 1), 0:192]).astype(bf16)
            ks[l, j] = both[:, 192:].astype(bf16)

        tick(l, 1)
        weights = keep_low(l, 1)
        keep = lax.broadcasted_iota(jnp.int32, (128, ROWS), 1) < FRAMES
        for j in range(2):
            vs[l, j] = (
                product(n1s[l], weights[j, :, 0:192]) + biases[j, pl.ds(3 * l, 1), 192:384]
            ).astype(bf16)

            def rows_of(r, carry, j=j):
                rows = pl.ds(pl.multiple_of(r * 128, 128), 128)
                heads = []
                for h in range(HEADS_HERE):
                    cols = slice(HEAD_DIM * h, HEAD_DIM * (h + 1))
                    scores = contract_last(qs[l, j, rows, cols], ks[l, j, :, cols]) * score_scale
                    scores = jnp.where(keep, scores, -1e30)
                    weight = jnp.exp(scores - jnp.max(scores, axis=-1, keepdims=True))
                    weight = weight * (1.0 / jnp.sum(weight, axis=-1, keepdims=True))
                    heads.append(product(weight.astype(bf16), vs[l, j, :, cols]))
                as_[l, j, rows, :] = jnp.concatenate(heads, axis=-1).astype(bf16)
                return carry

            lax.fori_loop(0, ROWS // 128, rows_of, 0)
        part[...] = contract_last(as_[l, 0], weights[0, :, 192:384])
        part[...] += contract_last(as_[l, 1], weights[1, :, 192:384])
        swap(0)
        ms[l] = hs[l] + (part[...] + other[0]) + params[4:5]
        scaled, _ = normalize_parts(ms[l])
        n2s[l] = (scaled * params[2:3] + params[3:4]).astype(bf16)

        for i in (2, 3):
            tick(l, i)
            weights = keep_low(l, i)

            @when(l > 0)
            def _(i=i):
                for copy in mid_copies(l - 1, i):
                    copy.wait()

            for j in range(2):
                before = product(n2s[l], weights[j]) + biases[j, pl.ds(3 * l + i - 1, 1), :]
                us[j, i - 2] = before
                cs[j, i - 2] = gelu(before).astype(bf16)
            for copy in mid_copies(l, i):
                copy.start()

        for i in (4, 5):
            tick(l, i)
            weights = keep_low(l, i)
            for j in range(2):
                term = contract_last(cs[j, i - 4], weights[j])
                if i == 4 and j == 0:
                    part[...] = term
                else:
                    part[...] += term
        swap(1)
        hs[l + 1] = ms[l] + (part[...] + other[1]) + params[5:6]
        for copy in out_copies(l):
            copy.start()
        return carry

    lax.fori_loop(0, LAYERS, layer, 0)

    last = LAYERS - 1
    for i in (2, 3):
        for copy in mid_copies(last, i):
            copy.wait()
    for l in range(LAYERS):
        for copy in out_copies(l):
            copy.wait()
    for slot in range(2):
        for j in range(2):
            local(low.at[slot, j], o_w.at[j, 0], low_sem.at[slot, j]).wait()
    wait_input(1)
    wait_input(2)

    @when(level < 3)
    def _():
        bias_copy(bias, 0, 0, p.above).wait_send()

    @when((level == 1) | (level == 2))
    def _():
        bias_copy(bias, 1, 1, p.above).wait_send()

    @when(level == 1)
    def _():
        bias_copy(bias, 1, 2, p.below).wait_send()

    def drain(u, carry):
        for j in range(2):

            @when((level < 3) if j == 0 else ((level == 1) | (level == 2)))
            def _(j=j):
                z_copy(gathered.at[j, u, p.q], u, j, p.above, sz.at[u, j]).wait_send()

            @when(level != j)
            def _(j=j):
                x_copy(u, j, p.q).wait_send()
                y_copy(u, j, p.q).wait_send()
                yd_copy(u, j, p.qx).wait_send()
                xd_copy(u, j, p.qy).wait_send()

        @when(level == 1)
        def _():
            z_copy(gathered.at[1, u, p.q], u, 1, p.below, szd.at[u]).wait_send()

        return carry

    lax.fori_loop(0, TOTAL, drain, 0)


def run_forward(frames, cotangent, wa, wm, bias, vectors):
    def hbm(shape, kind):
        return jax.ShapeDtypeStruct(shape, kind)

    dma = pltpu.SemaphoreType.DMA
    per_unit = dma((TOTAL, 2))
    return pl.pallas_call(
        forward_kernel,
        out_shape=(
            hbm((ROWS, WIDTH), f32),
            hbm((ROWS, WIDTH), f32),
            hbm((LAYERS, ROWS, WIDTH), f32),
            hbm((LAYERS, ROWS, WIDTH), f32),
            hbm((LAYERS, ROWS, WIDTH), bf16),
            hbm((LAYERS, ROWS, WIDTH), bf16),
            hbm((LAYERS, 2, ROWS, 192), bf16),
            hbm((LAYERS, 2, ROWS, 192), bf16),
            hbm((LAYERS, 2, ROWS, 192), bf16),
            hbm((LAYERS, 2, ROWS, 192), bf16),
            hbm((LAYERS, 2, 2, ROWS, BLOCK), f32),
            hbm((LAYERS, 2, 2, ROWS, BLOCK), bf16),
            hbm((2, TOTAL, WIDTH, BLOCK), bf16),
        ),
        in_specs=[ANY, ANY, ANY, ANY, ANY, VMEM],
        out_specs=(ANY,) * 13,
        scratch_shapes=[
            pltpu.VMEM((2, TOTAL, 4, 2, 96, BLOCK), f32),
            pltpu.VMEM((2, 8, BLOCK), f32),
            pltpu.VMEM((LAYERS + 1, ROWS, WIDTH), f32),
            pltpu.VMEM((LAYERS, ROWS, WIDTH), f32),
            pltpu.VMEM((LAYERS, ROWS, WIDTH), bf16),
            pltpu.VMEM((LAYERS, ROWS, WIDTH), bf16),
            pltpu.VMEM((LAYERS, 2, ROWS, 192), bf16),
            pltpu.VMEM((LAYERS, 2, ROWS, 192), bf16),
            pltpu.VMEM((LAYERS, 2, ROWS, 192), bf16),
            pltpu.VMEM((LAYERS, 2, ROWS, 192), bf16),
            pltpu.VMEM((2, 2, ROWS, BLOCK), f32),
            pltpu.VMEM((2, 2, ROWS, BLOCK), bf16),
            pltpu.VMEM((2, 2, WIDTH, BLOCK), bf16),
            pltpu.VMEM((ROWS, WIDTH), f32),
            pltpu.VMEM((2, ROWS, WIDTH), f32),
            per_unit,
            per_unit,
            dma((TOTAL,)),
            per_unit,
            per_unit,
            per_unit,
            per_unit,
            per_unit,
            per_unit,
            per_unit,
            per_unit,
            dma((TOTAL,)),
            dma((9,)),
            dma((6,)),
            dma((4,)),
            dma((2, 2)),
            dma((2, 2)),
            dma((8, LAYERS)),
        ],
        compiler_params=pltpu.CompilerParams(
            collective_id=0, has_side_effects=True, vmem_limit_bytes=63 << 20
        ),
        name="gather_forward",
    )(frames, cotangent, wa, wm, bias, vectors)


def reduce_kernel(
    grads,
    acts,
    o_fin,
    o_act,
    held,
    x1,
    y1,
    x2,
    y2,
    own,
    zin,
    zup,
    load_sem,
    sx1,
    rx1,
    sy1,
    ry1,
    sx2,
    rx2,
    sy2,
    ry2,
    szd,
    rzd,
    szu,
    rzu,
    sfin,
    rfin,
    lfin,
    act_send,
    act_recv,
    act_sem,
):
    p = find_place()
    greet(p)
    level = p.level
    when = pl.when

    def act_copy(src, j, n, k, device):
        return remote(src, o_act.at[j, n], act_send.at[n, k], act_recv.at[n, j], device)

    for n in range(3):

        @when(level == 0)
        def _(n=n):
            local(acts.at[n], o_act.at[0, n], act_sem.at[n]).start()
            act_copy(acts.at[n], 0, n, 0, p.above).start()

        @when(level == 1)
        def _(n=n):
            local(acts.at[n], o_act.at[1, n], act_sem.at[n]).start()
            act_copy(acts.at[n], 1, n, 1, p.above).start()
            act_copy(acts.at[n], 1, n, 2, p.below).start()

    def load(u):
        return local(grads.at[u], held.at[lax.rem(u, SLOTS)], load_sem.at[lax.rem(u, SLOTS)])

    def x1_copy(w):
        return remote(held.at[w, :, :, 1 - p.x, 0], x1.at[w], sx1.at[w], rx1.at[w], p.xn)

    def y1_copy(w):
        return remote(held.at[w, :, 1 - p.y, :, 1], y1.at[w], sy1.at[w], ry1.at[w], p.yn)

    def x2_copy(w):
        return remote(held.at[w, :, p.y, 1 - p.x, 1], x2.at[w], sx2.at[w], rx2.at[w], p.xn)

    def y2_copy(w):
        return remote(held.at[w, :, 1 - p.y, p.x, 0], y2.at[w], sy2.at[w], ry2.at[w], p.yn)

    def down_copy(u, j):
        return remote(own.at[u, j], zin.at[u, j], szd.at[u, j], rzd.at[u, j], p.below)

    def up_copy(u):
        return remote(own.at[u, 1], zup.at[u], szu.at[u], rzu.at[u], p.above)

    def fin_copy(u, j):
        return remote(own.at[u, j, 1 - p.c], o_fin.at[u], sfin.at[u], rfin.at[u], p.partner)

    def fin_local(u, j):
        return local(own.at[u, j, p.c], o_fin.at[u], lfin.at[u])

    def begin(u):
        w = lax.rem(u, SLOTS)

        @when(u >= SLOTS)
        def _():
            x1_copy(w).wait_send()
            y1_copy(w).wait_send()
            x2_copy(w).wait_send()
            y2_copy(w).wait_send()

        load(u).start()

    def stage_one(u):
        w = lax.rem(u, SLOTS)
        load(u).wait()
        x1_copy(w).start()
        y1_copy(w).start()

    def stage_two(u):
        w = lax.rem(u, SLOTS)
        x1_copy(w).wait_recv()
        held[w, :, 1 - p.y, p.x, 0] += x1[w, :, 1 - p.y]
        held[w, :, p.y, p.x, 0] += x1[w, :, p.y]
        y1_copy(w).wait_recv()
        held[w, :, p.y, 1 - p.x, 1] += y1[w, :, 1 - p.x]
        held[w, :, p.y, p.x, 1] += y1[w, :, p.x]
        y2_copy(w).start()
        x2_copy(w).start()

    def stage_three(u):
        w = lax.rem(u, SLOTS)
        y2_copy(w).wait_recv()
        own[u, :, 0] = held[w, :, p.y, p.x, 0] + y2[w]
        x2_copy(w).wait_recv()
        own[u, :, 1] = held[w, :, p.y, p.x, 1] + x2[w]

        @when(level == 3)
        def _():
            down_copy(u, 0).start()
            down_copy(u, 1).start()

        @when(level == 0)
        def _():
            up_copy(u).start()

    def level_two(u):
        for j in range(2):
            down_copy(u, j).wait_recv()
            own[u, j] += zin[u, j]
            down_copy(u, j).start()

    def level_one(u):
        down_copy(u, 0).wait_recv()
        own[u, 0] += zin[u, 0]
        down_copy(u, 0).start()
        down_copy(u, 1).wait_recv()
        up_copy(u).wait_recv()
        own[u, 1] += zin[u, 1] + zup[u]
        fin_local(u, 1).start()
        fin_copy(u, 1).start()

    def level_zero(u):
        down_copy(u, 0).wait_recv()
        own[u, 0] += zin[u, 0]
        fin_local(u, 0).start()
        fin_copy(u, 0).start()

    def in_range(u):
        return (u >= 0) & (u < TOTAL)

    def tick(s, carry):
        when(in_range(s + 1))(lambda: begin(s + 1))
        when(in_range(s))(lambda: stage_one(s))
        when(in_range(s - 1))(lambda: stage_two(s - 1))
        when(in_range(s - 2))(lambda: stage_three(s - 2))
        when(in_range(s - 3) & (level == 2))(lambda: level_two(s - 3))
        when(in_range(s - 4) & (level == 1))(lambda: level_one(s - 4))
        when(in_range(s - 5) & (level == 0))(lambda: level_zero(s - 5))
        for n in range(3):

            @when((s == 2 + 2 * n) & (level == 1))
            def _(n=n):
                act_copy(acts.at[n], 0, n, 0, p.above).wait_recv()
                act_copy(o_act.at[0, n], 0, n, 0, p.above).start()

            @when((s == 3 + 2 * n) & (level == 2))
            def _(n=n):
                act_copy(acts.at[n], 1, n, 1, p.above).wait_recv()
                act_copy(o_act.at[1, n], 1, n, 1, p.above).start()
                act_copy(acts.at[n], 0, n, 0, p.above).wait_recv()
                act_copy(o_act.at[0, n], 0, n, 0, p.above).start()

        return carry

    begin(0)
    lax.fori_loop(0, TOTAL + 5, tick, 0)

    for w in range(SLOTS):
        x1_copy(w).wait_send()
        y1_copy(w).wait_send()
        x2_copy(w).wait_send()
        y2_copy(w).wait_send()

    def drain(u, carry):
        @when(level > 0)
        def _():
            down_copy(u, 0).wait_send()

        @when(level > 1)
        def _():
            down_copy(u, 1).wait_send()
            fin_copy(u, 0).wait_recv()

        @when(level == 0)
        def _():
            up_copy(u).wait_send()

        @when(level < 2)
        def _():
            fin_local(u, 0).wait()
            fin_copy(u, 0).wait_send()

        return carry

    lax.fori_loop(0, TOTAL, drain, 0)
    for n in range(3):

        @when(level < 3)
        def _(n=n):
            act_copy(acts.at[n], 0, n, 0, p.above).wait_send()

        @when((level == 1) | (level == 2))
        def _(n=n):
            act_copy(acts.at[n], 1, n, 1, p.above).wait_send()

        @when(level == 1)
        def _(n=n):
            act_copy(acts.at[n], 1, n, 2, p.below).wait_send()

        @when(level < 2)
        def _(n=n):
            local(acts.at[n], o_act.at[0, n], act_sem.at[n]).wait()

        @when(level == 3)
        def _(n=n):
            act_copy(acts.at[n], 0, n, 0, p.above).wait_recv()

        @when((level == 0) | (level == 3))
        def _(n=n):
            act_copy(acts.at[n], 1, n, 1, p.above).wait_recv()


def run_reduce(grads, acts):
    dma = pltpu.SemaphoreType.DMA
    slots = dma((SLOTS,))
    units = dma((TOTAL,))
    return pl.pallas_call(
        reduce_kernel,
        out_shape=(
            jax.ShapeDtypeStruct((TOTAL, 96, BLOCK), f32),
            jax.ShapeDtypeStruct((2, 3, ROWS, WIDTH), f32),
        ),
        in_specs=[ANY, ANY],
        out_specs=(ANY, ANY),
        scratch_shapes=[
            pltpu.VMEM((SLOTS, 2, 2, 2, 2, 96, BLOCK), f32),
            pltpu.VMEM((SLOTS, 2, 2, 96, BLOCK), f32),
            pltpu.VMEM((SLOTS, 2, 2, 96, BLOCK), f32),
            pltpu.VMEM((SLOTS, 2, 96, BLOCK), f32),
            pltpu.VMEM((SLOTS, 2, 96, BLOCK), f32),
            pltpu.VMEM((TOTAL, 2, 2, 96, BLOCK), f32),
            pltpu.VMEM((TOTAL, 2, 2, 96, BLOCK), f32),
            pltpu.VMEM((TOTAL, 2, 96, BLOCK), f32),
            slots,
            slots,
            slots,
            slots,
            slots,
            slots,
            slots,
            slots,
            slots,
            dma((TOTAL, 2)),
            dma((TOTAL, 2)),
            units,
            units,
            units,
            units,
            units,
            dma((3, 3)),
            dma((3, 2)),
            dma((3,)),
        ],
        compiler_params=pltpu.CompilerParams(
            collective_id=1, has_side_effects=True, vmem_limit_bytes=60 << 20
        ),
        name="reduce_gradients",
    )(grads, acts)


def sum_cores(value):
    size = lax.axis_size("dp")
    return value + lax.ppermute(value, "dp", [(i, i + 1 - 2 * (i % 2)) for i in range(size)])


def backward(saved, vectors):
    x_in, cotangent, hs, ms, n1s, n2s, qs, ks, vs, as_, us, cs, low = saved
    keep = lax.broadcasted_iota(jnp.int32, (ROWS, ROWS), 1) < FRAMES
    upstream = cotangent
    units = []
    vector_grads = [None] * LAYERS
    head_grads = [None] * LAYERS
    up_grads = [None] * LAYERS
    for l in reversed(range(LAYERS)):
        params = vectors[l]
        base = UNITS * l
        scaled_two, inverse_two = normalize_parts(ms[l])
        scaled_one, inverse_one = normalize_parts(x_in if l == 0 else hs[l - 1])
        output_low = upstream.astype(bf16)
        down_bias_grad = jnp.sum(output_low.astype(f32), axis=0)
        for k in range(2):
            units.append(jnp.stack([contract_rows(output_low, cs[l, j, k]) for j in range(2)]))
        partial = 0.0
        up_rows = [[None, None], [None, None]]
        for k in range(2):
            pair = []
            for j in range(2):
                back = (product(output_low, low[j, base + 4 + k]) * gelu_slope(us[l, j, k])).astype(bf16)
                up_rows[j][k] = jnp.sum(back.astype(f32), axis=0)
                pair.append(contract_rows(n2s[l], back))
                partial = partial + contract_last(back, low[j, base + 2 + k])
            units.append(jnp.stack(pair))
        lowered, gain_two_grad, shift_two_grad = normalize_back(
            sum_cores(partial), scaled_two, inverse_two, params[2]
        )
        upstream = upstream + lowered
        branch_low = upstream.astype(bf16)
        out_bias_grad = jnp.sum(branch_low.astype(f32), axis=0)
        partial = 0.0
        vo_units, qk_units, head_rows = [], [], []
        for j in range(2):
            w_out = low[j, base + 1][:, 192:]
            out_grad = contract_rows(branch_low, as_[l, j])
            mixture_back = product(branch_low, w_out).astype(bf16)
            dq, dk, dv = [], [], []
            for h in range(HEADS_HERE):
                cols = slice(HEAD_DIM * h, HEAD_DIM * (h + 1))
                q, k, v, da = qs[l, j][:, cols], ks[l, j][:, cols], vs[l, j][:, cols], mixture_back[:, cols]
                scores = jnp.where(keep, contract_last(q, k) * score_scale, -1e30)
                weight = jnp.exp(scores - jnp.max(scores, axis=-1, keepdims=True))
                weight = weight * (1.0 / jnp.sum(weight, axis=-1, keepdims=True))
                prob_grad = contract_last(da, v)
                centre = jnp.sum(prob_grad * weight, axis=-1, keepdims=True)
                score_back = (weight * (prob_grad - centre)).astype(bf16)
                dq.append((product(score_back, k) * score_scale).astype(bf16))
                dk.append((contract_rows(score_back, q) * score_scale).astype(bf16))
                dv.append(contract_rows(weight.astype(bf16), da).astype(bf16))
            dq, dk, dv = (jnp.concatenate(parts, axis=-1) for parts in (dq, dk, dv))
            vo_units.append(jnp.concatenate([contract_rows(n1s[l], dv), out_grad], axis=-1))
            qk_units.append(
                jnp.concatenate([contract_rows(n1s[l], dq), contract_rows(n1s[l], dk)], axis=-1)
            )
            partial = (
                partial
                + contract_last(dq, low[j, base][:, :192])
                + contract_last(dk, low[j, base][:, 192:])
                + contract_last(dv, low[j, base + 1][:, :192])
            )
            head_rows.append((jnp.sum(dq.astype(f32), axis=0), jnp.sum(dv.astype(f32), axis=0)))
        units.append(jnp.stack(vo_units))
        units.append(jnp.stack(qk_units))
        lowered, gain_one_grad, shift_one_grad = normalize_back(
            sum_cores(partial), scaled_one, inverse_one, params[0]
        )
        upstream = upstream + lowered
        vector_grads[l] = jnp.stack(
            [gain_one_grad, shift_one_grad, gain_two_grad, shift_two_grad, out_bias_grad, down_bias_grad]
        )
        head_grads[l] = jnp.stack([jnp.stack([head_rows[j][n] for n in range(2)]) for j in range(2)])
        up_grads[l] = jnp.stack([jnp.concatenate(up_rows[j]) for j in range(2)])
    grads = jnp.stack(units).reshape(TOTAL, 2, 2, 2, 2, 96, BLOCK)
    return upstream, grads, jnp.stack(vector_grads), jnp.stack(head_grads), jnp.stack(up_grads)


def per_device(
    frames,
    cotangent,
    w_attn,
    w_mlp,
    vectors,
    head_bias,
    up_bias,
    moment_attn,
    square_attn,
    moment_mlp,
    square_mlp,
    moment_vectors,
    square_vectors,
    moment_head,
    square_head,
    moment_up,
    square_up,
):
    dp = lax.axis_index("dp")
    t = lax.axis_index("tensor")
    core = dp % 2
    dp_size = lax.axis_size("dp")

    def clips_of(block):
        return jnp.pad(block.reshape(2, FRAMES, WIDTH), ((0, 0), (0, ROWS - FRAMES), (0, 0)))

    wa = jnp.stack(
        [
            jnp.concatenate([w_attn[:, 0], w_attn[:, 1]], axis=-1),
            jnp.concatenate([w_attn[:, 2], w_attn[:, 3]], axis=-1),
        ],
        axis=1,
    ).reshape(LAYERS, 2, 4, 2, 96, BLOCK)
    wm = w_mlp.reshape(LAYERS, 2, 4, 2, 96, 2 * BLOCK)
    bias = jnp.concatenate(
        [head_bias.reshape(LAYERS, 1, BLOCK), up_bias.reshape(LAYERS, 2, BLOCK)], axis=1
    ).reshape(3 * LAYERS, BLOCK)
    bias = jnp.pad(bias, ((0, 8 - 3 * LAYERS), (0, 0)))
    saved = run_forward(clips_of(frames), clips_of(cotangent), wa, wm, bias, vectors)

    input_grad, grads, vector_grad, head_grad, up_grad = backward(saved, vectors)

    acts = jnp.concatenate([saved[2], input_grad[None]])
    fin, acts = run_reduce(grads, acts)

    acts = acts[:, :, :FRAMES]
    acts = jnp.where(core == 0, acts, acts[::-1])
    acts = jnp.concatenate([acts[0], acts[1]], axis=1)
    sections, upstream = acts[:2], acts[2]

    def in_order(pair, axis):
        return jnp.where(core == 0, pair, jnp.flip(pair, axis))

    head_grad = in_order(head_grad, 1).transpose(0, 2, 1, 3).reshape(LAYERS, 2, 2 * HEADS_HERE, HEAD_DIM)
    up_grad = in_order(up_grad, 1).reshape(LAYERS, 24, HEAD_DIM)
    head_all = jnp.concatenate(
        [jnp.where(core == k, head_grad, 0.0) for k in range(2)], axis=2
    )
    up_all = jnp.concatenate([jnp.where(core == k, up_grad, 0.0) for k in range(2)], axis=1)
    vector_all = jnp.where(core == 0, vector_grad, 0.0)
    vector_all, head_all, up_all = lax.psum((vector_all, head_all, up_all), ("dp", "tensor"))

    def owned(param, dim):
        size = param.shape[dim] // dp_size
        return lax.dynamic_slice_in_dim(param, dp * size, size, dim)

    head_all = lax.dynamic_slice_in_dim(head_all, t * HEADS_HERE, HEADS_HERE, 2)
    up_all = lax.dynamic_slice_in_dim(up_all, t * 12, 12, 1)

    if dp_size > GROUP:
        rows = jnp.zeros((TOTAL, WIDTH, BLOCK), f32)
        rows = lax.dynamic_update_slice_in_dim(rows, fin, (dp % GROUP) * 96, 1)
        fin = lax.psum_scatter(rows, "dp", scatter_dimension=1, tiled=True)

    def unit(l, k):
        return fin[(LAYERS - 1 - l) * UNITS + k]

    attn_grad = jnp.stack(
        [
            jnp.stack([unit(l, 5)[:, :192], unit(l, 5)[:, 192:], unit(l, 4)[:, :192], unit(l, 4)[:, 192:]])
            for l in range(LAYERS)
        ]
    )
    mlp_grad = jnp.stack(
        [
            jnp.stack(
                [
                    jnp.concatenate([unit(l, 2), unit(l, 3)], axis=-1),
                    jnp.concatenate([unit(l, 0), unit(l, 1)], axis=-1),
                ]
            )
            for l in range(LAYERS)
        ]
    )
    attn = adamw_update(owned(w_attn, 2), attn_grad, moment_attn, square_attn, rate_matrix)
    mlp = adamw_update(owned(w_mlp, 2), mlp_grad, moment_mlp, square_mlp, rate_matrix)
    vector_new = adamw_update(
        owned(vectors, 2), owned(vector_all, 2), moment_vectors, square_vectors, rate_vector
    )
    head = adamw_update(owned(head_bias, 3), owned(head_all, 3), moment_head, square_head, rate_vector)
    upper = adamw_update(owned(up_bias, 2), owned(up_all, 2), moment_up, square_up, rate_vector)
    return (sections, upstream, *attn, *mlp, *vector_new, *head, *upper)


def solution(mesh):
    in_specs = (
        P("dp", None),
        P("dp", None),
        P(None, None, None, "tensor"),
        P(None, None, None, "tensor"),
        P(),
        P(None, None, "tensor", None),
        P(None, "tensor", None),
        P(None, None, "dp", "tensor"),
        P(None, None, "dp", "tensor"),
        P(None, None, "dp", "tensor"),
        P(None, None, "dp", "tensor"),
        P(None, None, "dp"),
        P(None, None, "dp"),
        P(None, None, "tensor", "dp"),
        P(None, None, "tensor", "dp"),
        P(None, "tensor", "dp"),
        P(None, "tensor", "dp"),
    )
    out_specs = (
        P(None, "dp", None),
        P("dp", None),
        P(None, None, "dp", "tensor"),
        P(None, None, "dp", "tensor"),
        P(None, None, "dp", "tensor"),
        P(None, None, "dp", "tensor"),
        P(None, None, "dp", "tensor"),
        P(None, None, "dp", "tensor"),
        P(None, None, "dp"),
        P(None, None, "dp"),
        P(None, None, "dp"),
        P(None, None, "tensor", "dp"),
        P(None, None, "tensor", "dp"),
        P(None, None, "tensor", "dp"),
        P(None, "tensor", "dp"),
        P(None, "tensor", "dp"),
        P(None, "tensor", "dp"),
    )
    return jax.shard_map(
        per_device, mesh=mesh, in_specs=in_specs, out_specs=out_specs, check_vma=False
    )
```

time: 1350 us -> 952 us (0.71)
  waiting for transfers between devices: 968 us -> 108 us
  Pallas kernels: 0 us -> 475 us
  blocking collectives: 26 us -> 0 us
  other arithmetic: 83 us -> 101 us
    psum x7 -> x1, waiting for transfers between devices: 899 us -> 108 us  [per_device(): lax.psum((vector_all, head_all, up_all), ('dp', 'tensor'))]
    pallas_call x0 -> x2, Pallas kernels: none -> 475 us  [the longest x1 259 us: run_reduce(): pl.pallas_call(reduce_kernel, out_shape=(jax.ShapeDtypeStruct((TOTAL, 96,...]
    reduce_scatter x1 -> x0, waiting for transfers between devices: 67.8 us -> none  [per_device(): lax.psum_scatter(stacked[1], 'dp', scatter_dimension=2, tiled=True)]
    dot_general x24, matrix products: 84.5 us -> 25.5 us  [product(): return jnp.dot(left, right, preferred_element_type=f32)]
    dot_general x12 -> x56, matrix products: 19.8 us -> 58.1 us  [contract_rows(): lax.dot_general(left, right, (((0,), (0,)), ((), ())), preferred_element_...]
    unnamed x1 -> x0, blocking collectives: 26 us -> none
    unnamed x240 -> x371, local copies, waits for them, and re-layouts: 56.5 us -> 30.9 us
    unnamed x5 -> x11, other arithmetic: 0.01 us -> 22.9 us
  transfers between devices with their start and end apart: 10 -> 5, of which waited for: 9 -> 1; matrix products, arithmetic and copies ran while one was open for 7% -> 16% of each run, Pallas kernels for 0% -> 0%
where the time goes in v1:
time: 952 us; the launch traced here: 944 us
  Pallas kernels  475 us (50%)
  matrix products  135 us (14%)
  waiting for transfers between devices  108 us (11%)
  local copies, waits for them, and re-layouts  107 us (11%)
  other arithmetic  101 us (11%)
  between operations  16.4 us (2%)
    pallas_call x1, Pallas kernels, run_reduce(): pl.pallas_call(reduce_kernel, out_shape=(jax.ShapeDtypeStruct((TOTAL, 96,...  259 us
    pallas_call x1, Pallas kernels, run_forward(): pl.pallas_call(forward_kernel, out_shape=(hbm((ROWS, WIDTH), f32), hbm((R...  216 us
    psum x1, waiting for transfers between devices, per_device(): lax.psum((vector_all, head_all, up_all), ('dp', 'tensor'))  108 us
    dot_general x56, matrix products, contract_rows(): lax.dot_general(left, right, (((0,), (0,)), ((), ())), preferred_element_...  58.1 us
    dot_general x44, matrix products, contract_last(): lax.dot_general(left, right, (((1,), (1,)), ((), ())), preferred_element_...  51.3 us
    unnamed x371, local copies, waits for them, and re-layouts  30.9 us
    dot_general x24, matrix products, product(): return jnp.dot(left, right, preferred_element_type=f32)  25.5 us
    unnamed x11, other arithmetic  22.9 us
  transfers between devices with their start and end apart: 5, of which 1 were waited for; matrix products, arithmetic and copies ran while one was open for 16% of the time, Pallas kernels for 0%

profile of v1, /device:TPU:0, one launch (start us, length us, event | category | flops | bytes accessed | tf_op | source)
XLA Modules:
  0.0 943.8 jit_solution(10075167889913591486)
XLA Ops:
  7.2 3.8 fusion.431
  11.0 2.9 copy.104
  30.3 4.6 maximum_maximum_fusion.wa
  35.0 216.3 %gather_forward.1 = (f32[512,768]{1,0:T(8,128)}, f32[512,768]{1,0:T(8,128)}, f32[2,512,768]{2,1,0:T(8,128)}, f32[2,512,768]{2,1,0:T(8,128)}, bf16[2,512,768]{2,1...) custom-call(f32[2,512,768]{2,1,0:T(8,128)} %pad.11.frames, ...), custom_call_target="tpu_custom_call" | custom-call | tf_op jit(solution)/shard_map/gather_forward/pallas_call | solution.py:557
  266.5 2.9 add_add_fusion.3
  332.2 3.4 maximum_dynamic-update-slice_fusion.11
  345.1 4.1 slice_bitcast_fusion.5
  349.1 3.5 multiply_reduce_fusion
  403.2 3.3 maximum_dynamic-update-slice_fusion.7
  409.3 3.5 multiply_reduce_fusion.1
  415.1 3.1 convert_reduce_fusion.10
  423.7 3.0 convert_reduce_fusion.9
  429.0 2.9 convolution_bitcast_fusion.5
  442.7 3.0 add_add_fusion.1
  463.0 3.4 multiply_reduce_fusion.2
  497.0 3.6 add_add_fusion
  517.3 3.4 maximum_dynamic-update-slice_fusion.1
  529.7 258.6 %reduce_gradients.1 = (f32[12,96,384]{2,1,0:T(8,128)}, f32[2,3,512,768]{3,2,1,0:T(8,128)}) custom-call(f32[12,2,2,2,2,96,384]{6,5,4,3,2,1,0:T(8,128)} %maximum_dynamic-update-slice_fusion.grads, f32[3,512,768]{2,1,0:T(8,128)} %pad_maximum_fusion.acts), custom_call_target="tpu_custom_call" | custom-call | tf_op jit(solution)/shard_map/reduce_gradients/pallas_call | solution.py:855
  793.5 4.2 slice.677
  798.4 4.2 slice_bitcast_fusion
  805.6 5.1 fusion
  810.8 3.8 multiply_subtract_fusion
  817.9 3.8 fusion.1
  821.7 108.3 %all-reduce.6.cloned.1.call-done = (f32[2,6,768]{2,1,0:T(8,128)}, f32[2,2,12,64]{3,2,1,0:T(8,128)}, f32[2,48,64]{1,2,0:T(8,128)}) async-done(((f32[2,6,768]{2,1,0:T(8,128)}, f32[2,2,12,64]{3,2,1,0:T(8,128)}, f32[2,48,64]{1,2,0:T(8,128)}), (f32[2,6,768]{2,1,0:T(8,128)}, f32[2,2,12,64]{3,2,1,0:T(8,128)}, f32[2,48,64]{1,2,0:T(8,128)})) %all-reduce.6.cloned.1.call-update) | async-done | bytes 73744 | tf_op jit(solution)/shard_map/psum | solution.py:1044
  (686 shorter events, 268.8 us)
Async XLA Ops:
  7.2 922.7 %all-reduce.6.cloned.1.call-start = ((), (), s32[]{:S(2)}) async-start(), calls=%async_computation | async-start | bytes 294912 | tf_op jit(solution)/shard_map/psum | solution.py:1044
  269.4 79.7 %collective-permute-start = (f32[512,768]{1,0:T(8,128)}, f32[512,768]{1,0:T(8,128)}, u32[]{:S(2)}, u32[]{:S(2)}) collective-permute-start(f32[512,768]{1,0:T(8,128)} %add_add_fusion.3), channel_id=1, source_target_pairs={{0,4},{4,0},{8,12},{12,8},{16,20},{20,16},{24,28},{28,24},{1,5},{5... | collective-permute-start | bytes 4718600 | tf_op jit(solution)/shard_map/ppermute | solution.py:901
  270.2 16.4 %copy-start.61 = (bf16[512,192]{1,0:T(8,128)(2,1)}, bf16[512,192]{1,0:T(8,128)(2,1)S(1)}, u32[]{:S(2)}) copy-start(bf16[512,192]{1,0:T(8,128)(2,1)S(1)} %get-tuple-element.170) | copy-start | bytes 589828
  278.6 86.3 %copy-start.135 = (f32[512]{0:T(512)}, f32[512]{0:T(512)S(1)}, u32[]{:S(2)}) copy-start(f32[512]{0:T(512)S(1)} %get-tuple-element.191) | copy-start | bytes 6148
  279.9 86.6 %copy-start.133 = (f32[512]{0:T(512)}, f32[512]{0:T(512)S(1)}, u32[]{:S(2)}) copy-start(f32[512]{0:T(512)S(1)} %get-tuple-element.189) | copy-start | bytes 6148
  281.3 34.0 %copy-start.131 = (f32[512]{0:T(512)}, f32[512]{0:T(512)S(1)}, u32[]{:S(2)}) copy-start(f32[512]{0:T(512)S(1)} %get-tuple-element.223) | copy-start | bytes 6148
  282.7 33.5 %copy-start.129 = (f32[512]{0:T(512)}, f32[512]{0:T(512)S(1)}, u32[]{:S(2)}) copy-start(f32[512]{0:T(512)S(1)} %get-tuple-element.221) | copy-start | bytes 6148
  284.0 44.8 %copy-start.127 = (f32[512]{0:T(512)}, f32[512]{0:T(512)S(1)}, u32[]{:S(2)}) copy-start(f32[512]{0:T(512)S(1)} %get-tuple-element.219) | copy-start | bytes 6148
  285.3 45.1 %copy-start.125 = (f32[512]{0:T(512)}, f32[512]{0:T(512)S(1)}, u32[]{:S(2)}) copy-start(f32[512]{0:T(512)S(1)} %get-tuple-element.217) | copy-start | bytes 6148
  309.8 39.4 %copy-start.144 = (f32[512]{0:T(512)}, f32[512]{0:T(512)S(1)}, u32[]{:S(2)}) copy-start(f32[512]{0:T(512)S(1)} %get-tuple-element.257) | copy-start | bytes 6148
  312.6 52.4 %copy-start.155 = (f32[512]{0:T(512)}, f32[512]{0:T(512)S(1)}, u32[]{:S(2)}) copy-start(f32[512]{0:T(512)S(1)} %broadcast_divide_fusion.7) | copy-start | bytes 6148
  313.0 53.5 %copy-start.157 = (f32[512]{0:T(512)}, f32[512]{0:T(512)S(1)}, u32[]{:S(2)}) copy-start(f32[512]{0:T(512)S(1)} %broadcast_divide_fusion.6) | copy-start | bytes 6148
  377.8 31.0 %collective-permute-start.1 = (f32[512,768]{1,0:T(8,128)}, f32[512,768]{1,0:T(8,128)}, u32[]{:S(2)}, u32[]{:S(2)}) collective-permute-start(f32[512,768]{1,0:T(8,128)} %add_add_fusion.2), channel_id=1, source_target_pairs={{0,4},{4,0},{8,12},{12,8},{16,20},{20,16},{24,28},{28,24},{1,5},{5... | collective-permute-start | bytes 4718600 | tf_op jit(solution)/shard_map/ppermute | solution.py:901
  445.6 17.4 %collective-permute-start.2 = (f32[512,768]{1,0:T(8,128)}, f32[512,768]{1,0:T(8,128)}, u32[]{:S(2)}, u32[]{:S(2)}) collective-permute-start(f32[512,768]{1,0:T(8,128)} %add_add_fusion.1), channel_id=1, source_target_pairs={{0,4},{4,0},{8,12},{12,8},{16,20},{20,16},{24,28},{28,24},{1,5},{5... | collective-permute-start | bytes 4718600 | tf_op jit(solution)/shard_map/ppermute | solution.py:901
  476.7 20.0 %copy-start.100 = (bf16[512,64]{0,1:T(8,128)(2,1)}, bf16[512,64]{0,1:T(8,128)(2,1)S(1)}, u32[]{:S(2)}) copy-start(bf16[512,64]{0,1:T(8,128)(2,1)S(1)} %convolution_convert_fusion.4) | copy-start | bytes 196612
  500.7 21.7 %collective-permute-start.3 = (f32[512,768]{1,0:T(8,128)S(1)}, f32[512,768]{1,0:T(8,128)}, u32[]{:S(2)}, u32[]{:S(2)}) collective-permute-start(f32[512,768]{1,0:T(8,128)S(1)} %add_add_fusion), channel_id=1, source_target_pairs={{0,4},{4,0},{8,12},{12,8},{16,20},{20,16},{24,28},{28,24},{1,5},{5... | collective-permute-start | bytes 4718600 | tf_op jit(solution)/shard_map/ppermute | solution.py:901
  817.8 112.1 %copy-start.123 = (f32[2,2,3,64]{3,2,1,0:T(4,128)S(1)}, f32[2,2,3,64]{3,2,1,0:T(4,128)}, u32[]{:S(2)}) copy-start(f32[2,2,3,64]{3,2,1,0:T(4,128)} %copy-done.122) | copy-start | bytes 9220
  817.8 112.1 %copy-start.174 = (f32[2,2,3,8]{3,1,2,0:T(2,128)S(1)}, f32[2,2,3,8]{3,1,2,0:T(2,128)}, u32[]{:S(2)}) copy-start(f32[2,2,3,8]{3,1,2,0:T(2,128)} %param.30) | copy-start | bytes 1156
  817.8 112.1 %copy-start.175 = (f32[2,2,3,8]{3,1,2,0:T(2,128)S(1)}, f32[2,2,3,8]{3,1,2,0:T(2,128)}, u32[]{:S(2)}) copy-start(f32[2,2,3,8]{3,1,2,0:T(2,128)} %param.31) | copy-start | bytes 1156
  817.8 114.8 %copy-start.176 = (f32[2,6,96]{2,0,1:T(2,128)S(1)}, f32[2,6,96]{2,0,1:T(2,128)}, u32[]{:S(2)}) copy-start(f32[2,6,96]{2,0,1:T(2,128)} %param.28) | copy-start | bytes 13828
  817.8 114.8 %copy-start.177 = (f32[2,6,96]{2,0,1:T(2,128)S(1)}, f32[2,6,96]{2,0,1:T(2,128)}, u32[]{:S(2)}) copy-start(f32[2,6,96]{2,0,1:T(2,128)} %param.29) | copy-start | bytes 13828
  817.8 117.4 %copy-start.148 = (f32[2,12,8]{1,2,0:T(8,128)S(1)}, f32[2,12,8]{1,2,0:T(8,128)}, u32[]{:S(2)}) copy-start(f32[2,12,8]{1,2,0:T(8,128)} %copy.157) | copy-start | bytes 2308
  817.8 117.4 %copy-start.169 = (f32[2,12,8]{1,2,0:T(8,128)S(1)}, f32[2,12,8]{1,2,0:T(8,128)}, u32[]{:S(2)}) copy-start(f32[2,12,8]{1,2,0:T(8,128)} %param.32) | copy-start | bytes 2308
  817.9 117.4 %copy-start.170 = (f32[2,12,8]{1,2,0:T(8,128)S(1)}, f32[2,12,8]{1,2,0:T(8,128)}, u32[]{:S(2)}) copy-start(f32[2,12,8]{1,2,0:T(8,128)} %param.33) | copy-start | bytes 2308
  (161 other events, 427.8 us)
Sparse Core Ops, SparseCore 0:
  810.8 119.0 all-reduce.5

commit v2 on v1

--- a/solution.py
+++ b/solution.py
@@ -19,7 +19,7 @@
 TOTAL = LAYERS * UNITS
 GROUP = 8
 HEADS_HERE = 3
-SLOTS = 4
+SLOTS = 3
 
 ln_eps = 1e-05
 beta_one = 0.9
@@ -171,7 +171,6 @@
     wm,
     bias,
     vec,
-    o_x,
     o_ct,
     o_h,
     o_m,
@@ -227,7 +226,7 @@
 
     mine = (p.t // 2) == p.c
     clip = lax.rem(p.t, 2)
-    inputs = ((frames, hs.at[0], 0), (frames, o_x, 1), (cotangent, o_ct, 2))
+    inputs = ((frames, hs.at[0], 0), (frames, o_h.at[0], 1), (cotangent, o_ct, 2))
 
     @when(mine)
     def _():
@@ -409,7 +408,7 @@
 
     def out_copies(l):
         return [
-            local(hs.at[l + 1], o_h.at[l], out_sem.at[0, l]),
+            local(hs.at[l + 1], o_h.at[l + 1], out_sem.at[0, l]),
             local(ms.at[l], o_m.at[l], out_sem.at[1, l]),
             local(n1s.at[l], o_n1.at[l], out_sem.at[2, l]),
             local(n2s.at[l], o_n2.at[l], out_sem.at[3, l]),
@@ -558,8 +557,7 @@
         forward_kernel,
         out_shape=(
             hbm((ROWS, WIDTH), f32),
-            hbm((ROWS, WIDTH), f32),
-            hbm((LAYERS, ROWS, WIDTH), f32),
+            hbm((LAYERS + 1, ROWS, WIDTH), f32),
             hbm((LAYERS, ROWS, WIDTH), f32),
             hbm((LAYERS, ROWS, WIDTH), bf16),
             hbm((LAYERS, ROWS, WIDTH), bf16),
@@ -572,7 +570,7 @@
             hbm((2, TOTAL, WIDTH, BLOCK), bf16),
         ),
         in_specs=[ANY, ANY, ANY, ANY, ANY, VMEM],
-        out_specs=(ANY,) * 13,
+        out_specs=(ANY,) * 12,
         scratch_shapes=[
             pltpu.VMEM((2, TOTAL, 4, 2, 96, BLOCK), f32),
             pltpu.VMEM((2, 8, BLOCK), f32),
@@ -615,11 +613,23 @@
     )(frames, cotangent, wa, wm, bias, vectors)
 
 
-def reduce_kernel(
-    grads,
-    acts,
+def backward_kernel(
+    i_ct,
+    i_h,
+    i_m,
+    i_n1,
+    i_n2,
+    i_q,
+    i_k,
+    i_v,
+    i_a,
+    i_u,
+    i_c,
+    i_w,
+    vec,
     o_fin,
     o_act,
+    o_small,
     held,
     x1,
     y1,
@@ -628,7 +638,25 @@
     own,
     zin,
     zup,
-    load_sem,
+    grad,
+    part,
+    other,
+    h_in,
+    m_in,
+    n1,
+    n2,
+    q,
+    k,
+    v,
+    a,
+    u_in,
+    c_in,
+    w_in,
+    low,
+    dqk,
+    dv,
+    small,
+    small_in,
     sx1,
     rx1,
     sy1,
@@ -647,30 +675,52 @@
     act_send,
     act_recv,
     act_sem,
+    load_sem,
+    unit_sem,
+    swap_sem,
+    small_send,
+    small_recv,
+    ct_sem,
 ):
     p = find_place()
     greet(p)
     level = p.level
     when = pl.when
 
-    def act_copy(src, j, n, k, device):
-        return remote(src, o_act.at[j, n], act_send.at[n, k], act_recv.at[n, j], device)
-
-    for n in range(3):
+    def act_copy(src, j, n, m, device):
+        return remote(src, o_act.at[j, n], act_send.at[n, m], act_recv.at[n, j], device)
+
+    def act_source(n):
+        return i_h.at[n + 1] if n < LAYERS else grad
+
+    def act_begin(n):
+        src = act_source(n)
 
         @when(level == 0)
-        def _(n=n):
-            local(acts.at[n], o_act.at[0, n], act_sem.at[n]).start()
-            act_copy(acts.at[n], 0, n, 0, p.above).start()
+        def _():
+            local(src, o_act.at[0, n], act_sem.at[n]).start()
+            act_copy(src, 0, n, 0, p.above).start()
 
         @when(level == 1)
-        def _(n=n):
-            local(acts.at[n], o_act.at[1, n], act_sem.at[n]).start()
-            act_copy(acts.at[n], 1, n, 1, p.above).start()
-            act_copy(acts.at[n], 1, n, 2, p.below).start()
-
-    def load(u):
-        return local(grads.at[u], held.at[lax.rem(u, SLOTS)], load_sem.at[lax.rem(u, SLOTS)])
+        def _():
+            local(src, o_act.at[1, n], act_sem.at[n]).start()
+            act_copy(src, 1, n, 1, p.above).start()
+            act_copy(src, 1, n, 2, p.below).start()
+
+    def act_pass(n, at, s):
+        src = act_source(n)
+
+        @when((s == at) & (level == 1))
+        def _():
+            act_copy(src, 0, n, 0, p.above).wait_recv()
+            act_copy(o_act.at[0, n], 0, n, 0, p.above).start()
+
+        @when((s == at + 1) & (level == 2))
+        def _():
+            act_copy(src, 1, n, 1, p.above).wait_recv()
+            act_copy(o_act.at[1, n], 1, n, 1, p.above).start()
+            act_copy(src, 0, n, 0, p.above).wait_recv()
+            act_copy(o_act.at[0, n], 0, n, 0, p.above).start()
 
     def x1_copy(w):
         return remote(held.at[w, :, :, 1 - p.x, 0], x1.at[w], sx1.at[w], rx1.at[w], p.xn)
@@ -696,26 +746,17 @@
     def fin_local(u, j):
         return local(own.at[u, j, p.c], o_fin.at[u], lfin.at[u])
 
-    def begin(u):
-        w = lax.rem(u, SLOTS)
-
-        @when(u >= SLOTS)
-        def _():
-            x1_copy(w).wait_send()
-            y1_copy(w).wait_send()
-            x2_copy(w).wait_send()
-            y2_copy(w).wait_send()
-
-        load(u).start()
-
-    def stage_one(u):
-        w = lax.rem(u, SLOTS)
-        load(u).wait()
+    def sent(w):
+        x1_copy(w).wait_send()
+        y1_copy(w).wait_send()
+        x2_copy(w).wait_send()
+        y2_copy(w).wait_send()
+
+    def stage_one(w):
         x1_copy(w).start()
         y1_copy(w).start()
 
-    def stage_two(u):
-        w = lax.rem(u, SLOTS)
+    def stage_two(w):
         x1_copy(w).wait_recv()
         held[w, :, 1 - p.y, p.x, 0] += x1[w, :, 1 - p.y]
         held[w, :, p.y, p.x, 0] += x1[w, :, p.y]
@@ -725,8 +766,7 @@
         y2_copy(w).start()
         x2_copy(w).start()
 
-    def stage_three(u):
-        w = lax.rem(u, SLOTS)
+    def stage_three(u, w):
         y2_copy(w).wait_recv()
         own[u, :, 0] = held[w, :, p.y, p.x, 0] + y2[w]
         x2_copy(w).wait_recv()
@@ -763,41 +803,270 @@
         fin_local(u, 0).start()
         fin_copy(u, 0).start()
 
-    def in_range(u):
-        return (u >= 0) & (u < TOTAL)
-
-    def tick(s, carry):
-        when(in_range(s + 1))(lambda: begin(s + 1))
-        when(in_range(s))(lambda: stage_one(s))
-        when(in_range(s - 1))(lambda: stage_two(s - 1))
-        when(in_range(s - 2))(lambda: stage_three(s - 2))
-        when(in_range(s - 3) & (level == 2))(lambda: level_two(s - 3))
-        when(in_range(s - 4) & (level == 1))(lambda: level_one(s - 4))
-        when(in_range(s - 5) & (level == 0))(lambda: level_zero(s - 5))
-        for n in range(3):
-
-            @when((s == 2 + 2 * n) & (level == 1))
-            def _(n=n):
-                act_copy(acts.at[n], 0, n, 0, p.above).wait_recv()
-                act_copy(o_act.at[0, n], 0, n, 0, p.above).start()
-
-            @when((s == 3 + 2 * n) & (level == 2))
-            def _(n=n):
-                act_copy(acts.at[n], 1, n, 1, p.above).wait_recv()
-                act_copy(o_act.at[1, n], 1, n, 1, p.above).start()
-                act_copy(acts.at[n], 0, n, 0, p.above).wait_recv()
-                act_copy(o_act.at[0, n], 0, n, 0, p.above).start()
-
+    def service(s, i):
+        if isinstance(s, int):
+
+            def guard(ok, step):
+                if ok:
+                    step()
+        else:
+
+            def guard(ok, step):
+                when(ok)(step)
+
+        if isinstance(s, int):
+            assert s >= TOTAL
+        else:
+            stage_one(i % SLOTS)
+        guard((s >= 1) & (s - 1 < TOTAL), lambda: stage_two((i - 1) % SLOTS))
+        guard((s >= 2) & (s - 2 < TOTAL), lambda: stage_three(s - 2, (i - 2) % SLOTS))
+        guard((s >= 3) & (s - 3 < TOTAL), lambda: when(level == 2)(lambda: level_two(s - 3)))
+        guard((s >= 4) & (s - 4 < TOTAL), lambda: when(level == 1)(lambda: level_one(s - 4)))
+        guard((s >= 5) & (s - 5 < TOTAL), lambda: when(level == 0)(lambda: level_zero(s - 5)))
+
+    def loads(l):
+        whole = (
+            (i_c, c_in),
+            (i_u, u_in),
+            (i_n2, n2),
+            (i_m, m_in),
+            (i_a, a),
+            (i_q, q),
+            (i_k, k),
+            (i_v, v),
+            (i_n1, n1),
+            (i_h, h_in),
+        )
+        return [local(src.at[l], dst, load_sem.at[n]) for n, (src, dst) in enumerate(whole)]
+
+    def unit_load(l, i):
+        return local(i_w.at[:, UNITS * l + i], w_in.at[:, i], unit_sem.at[i])
+
+    def swap(slot):
+        copy = remote(part, other.at[slot], swap_sem.at[slot], swap_sem.at[2 + slot], p.partner)
+        copy.start()
+        copy.wait()
+
+    def put(w, j, value):
+        held[w, j] = value.reshape(2, 2, 2, 96, BLOCK)
+
+    def small_row(l, row, value):
+        small[l, row : row + 1] = value[:, :BLOCK]
+        small[l, row + 1 : row + 2] = value[:, BLOCK:]
+
+    def norm_back(slot, l, source, gain, first):
+        def rows_of(r, carry):
+            rows = pl.ds(pl.multiple_of(r * 128, 128), 128)
+            upstream = part[rows] + other[slot, rows]
+            scaled, inverse = normalize_parts(source[rows])
+            lowered, gain_grad, shift_grad = normalize_back(upstream, scaled, inverse, gain)
+            value = grad[rows] + lowered
+            grad[rows] = value
+            rounded = value.astype(bf16)
+            low[rows] = rounded
+            bias_grad = jnp.sum(rounded.astype(f32), axis=0)
+            return (
+                carry[0] + gain_grad.reshape(1, WIDTH),
+                carry[1] + shift_grad.reshape(1, WIDTH),
+                carry[2] + bias_grad.reshape(1, WIDTH),
+            )
+
+        zero = jnp.zeros((1, WIDTH), f32)
+        sums = lax.fori_loop(0, ROWS // 128, rows_of, (zero, zero, zero))
+        small_row(l, first, sums[0])
+        small_row(l, first + 2, sums[1])
+        return sums[2]
+
+    keep = lax.broadcasted_iota(jnp.int32, (ROWS, ROWS), 1) < FRAMES
+
+    def attention_back(j, carry):
+        mixture_back = product(low[...], w_in[j, 1, :, 192:384]).astype(bf16)
+        parts = ([], [], [])
+        for h in range(HEADS_HERE):
+            cols = slice(HEAD_DIM * h, HEAD_DIM * (h + 1))
+            qh, kh, vh, dah = q[j, :, cols], k[j, :, cols], v[j, :, cols], mixture_back[:, cols]
+            scores = jnp.where(keep, contract_last(qh, kh) * score_scale, -1e30)
+            weight = jnp.exp(scores - jnp.max(scores, axis=-1, keepdims=True))
+            weight = weight * (1.0 / jnp.sum(weight, axis=-1, keepdims=True))
+            prob_grad = contract_last(dah, vh)
+            centre = jnp.sum(prob_grad * weight, axis=-1, keepdims=True)
+            score_back = (weight * (prob_grad - centre)).astype(bf16)
+            parts[0].append((product(score_back, kh) * score_scale).astype(bf16))
+            parts[1].append((contract_rows(score_back, qh) * score_scale).astype(bf16))
+            parts[2].append(contract_rows(weight.astype(bf16), dah).astype(bf16))
+        dqk[j] = jnp.concatenate(parts[0] + parts[1], axis=-1)
+        dv[j] = jnp.concatenate(parts[2], axis=-1)
         return carry
 
-    begin(0)
-    lax.fori_loop(0, TOTAL + 5, tick, 0)
+    local(i_ct, grad, ct_sem.at[0]).start()
+
+    def layer(step, carry):
+        l = LAYERS - 1 - step
+        s0 = UNITS * step
+        params = vec[l]
+        fetch = loads(l)
+        for copy in fetch[:2]:
+            copy.start()
+        for i in (4, 5, 2, 3):
+            unit_load(l, i).start()
+        for copy in fetch[2:]:
+            copy.start()
+        for i in (1, 0):
+            unit_load(l, i).start()
+
+        def free(s, w):
+            when(s >= SLOTS)(lambda: sent(w))
+
+        @when(step == 0)
+        def _():
+            local(i_ct, grad, ct_sem.at[0]).wait()
+            low[...] = grad[...].astype(bf16)
+            small_row(l, 10, jnp.sum(low[...].astype(f32), axis=0, keepdims=True))
+
+        fetch[0].wait()
+        for i in (0, 1):
+            free(s0 + i, i)
+            for j in range(2):
+                put(i, j, contract_rows(low[...], c_in[j, i]))
+            service(s0 + i, i)
+            if i == 0:
+
+                @when(step == 0)
+                def _():
+                    act_begin(0)
+                    act_begin(1)
+
+        fetch[1].wait()
+        fetch[2].wait()
+        for i in (2, 3):
+            h = i - 2
+            unit_load(l, 4 + h).wait()
+            unit_load(l, 2 + h).wait()
+            w = i % SLOTS
+            free(s0 + i, w)
+            for j in range(2):
+                back = (product(low[...], w_in[j, 4 + h]) * gelu_slope(u_in[j, h])).astype(bf16)
+                row = 14 + 2 * j + h
+                small[l, row : row + 1] = jnp.sum(back.astype(f32), axis=0, keepdims=True)
+                put(w, j, contract_rows(n2[...], back))
+                term = contract_last(back, w_in[j, 2 + h])
+                if h == 0 and j == 0:
+                    part[...] = term
+                else:
+                    part[...] += term
+            service(s0 + i, i)
+        swap(0)
+        fetch[3].wait()
+        small_row(l, 8, norm_back(0, l, m_in, params[2:3], 4))
+
+        for copy in fetch[4:]:
+            copy.wait()
+        unit_load(l, 1).wait()
+        unit_load(l, 0).wait()
+        lax.fori_loop(0, 2, attention_back, 0)
+        free(s0 + 4, 4 % SLOTS)
+        for j in range(2):
+            held[4 % SLOTS, j, :, :, :, :, 0:192] = contract_rows(n1[...], dv[j]).reshape(2, 2, 2, 96, 192)
+            held[4 % SLOTS, j, :, :, :, :, 192:384] = contract_rows(low[...], a[j]).reshape(2, 2, 2, 96, 192)
+        service(s0 + 4, 4)
+        free(s0 + 5, 5 % SLOTS)
+        for j in range(2):
+            put(5 % SLOTS, j, contract_rows(n1[...], dqk[j]))
+            sums = jnp.sum(dqk[j].astype(f32), axis=0, keepdims=True)
+            small[l, 12 + j : 13 + j, 0:192] = sums[:, 0:192]
+            small[l, 12 + j : 13 + j, 192:384] = jnp.sum(dv[j].astype(f32), axis=0, keepdims=True)
+            term = contract_last(dqk[j], w_in[j, 0]) + contract_last(dv[j], w_in[j, 1, :, 0:192])
+            if j == 0:
+                part[...] = term
+            else:
+                part[...] += term
+        service(s0 + 5, 5)
+        swap(1)
+        down_sum = norm_back(1, l, h_in, params[0:1], 0)
+
+        @when(l > 0)
+        def _():
+            small_row(l - 1, 10, down_sum)
+
+        for n in range(LAYERS):
+            act_pass(n, 0, step - n)
+
+        return carry
+
+    small[...] = jnp.zeros_like(small)
+    lax.fori_loop(0, LAYERS, layer, 0)
+
+    def small_copy(m, device):
+        return remote(small, small_in.at[m], small_send.at[m], small_recv.at[m], device)
+
+    def small_step(m, device):
+        copy = small_copy(m, device)
+        copy.start()
+        return copy
+
+    act_begin(2)
+    act_pass(1, -1, 0)
+    small_copy(0, p.xn).start()
+    service(TOTAL, 0)
+    small_copy(0, p.xn).wait()
+    small[...] += small_in[0]
+    small_copy(1, p.yn).start()
+    act_pass(2, 0, 0)
+    service(TOTAL + 1, 1)
+    small_copy(1, p.yn).wait()
+    small[...] += small_in[1]
+
+    @when((level == 0) | (level == 2))
+    def _():
+        small_copy(2, p.above).start()
+
+    @when((level == 1) | (level == 3))
+    def _():
+        small_copy(2, p.below).start()
+
+    act_pass(2, -1, 0)
+    service(TOTAL + 2, 2)
+    small_copy(2, p.above).wait()
+    small[...] += small_in[2]
+
+    @when(level == 1)
+    def _():
+        small_copy(3, p.above).start()
+
+    @when(level == 2)
+    def _():
+        small_copy(3, p.below).start()
+
+    service(TOTAL + 3, 3)
+
+    @when(level == 1)
+    def _():
+        small_copy(3, p.above).wait()
+        small[...] += small_in[3]
+        small_copy(4, p.below).start()
+        small_copy(4, p.below).wait_send()
+
+    @when(level == 2)
+    def _():
+        small_copy(3, p.below).wait()
+        small[...] += small_in[3]
+        small_copy(4, p.above).start()
+        small_copy(4, p.above).wait_send()
+
+    service(TOTAL + 4, 4)
+
+    @when((level == 0) | (level == 3))
+    def _():
+        small_copy(4, p.above).wait_recv()
+        small[...] = small_in[4]
+
+    small_copy(5, p.partner).start()
+    local(small, o_small.at[0], ct_sem.at[1]).start()
+    small_copy(5, p.partner).wait()
+    local(small_in.at[5], o_small.at[1], ct_sem.at[2]).start()
 
     for w in range(SLOTS):
-        x1_copy(w).wait_send()
-        y1_copy(w).wait_send()
-        x2_copy(w).wait_send()
-        y2_copy(w).wait_send()
+        sent(w)
 
     def drain(u, carry):
         @when(level > 0)
@@ -822,44 +1091,53 @@
 
     lax.fori_loop(0, TOTAL, drain, 0)
     for n in range(3):
+        src = act_source(n)
 
         @when(level < 3)
-        def _(n=n):
-            act_copy(acts.at[n], 0, n, 0, p.above).wait_send()
+        def _(n=n, src=src):
+            act_copy(src, 0, n, 0, p.above).wait_send()
 
         @when((level == 1) | (level == 2))
-        def _(n=n):
-            act_copy(acts.at[n], 1, n, 1, p.above).wait_send()
+        def _(n=n, src=src):
+            act_copy(src, 1, n, 1, p.above).wait_send()
 
         @when(level == 1)
-        def _(n=n):
-            act_copy(acts.at[n], 1, n, 2, p.below).wait_send()
+        def _(n=n, src=src):
+            act_copy(src, 1, n, 2, p.below).wait_send()
 
         @when(level < 2)
-        def _(n=n):
-            local(acts.at[n], o_act.at[0, n], act_sem.at[n]).wait()
+        def _(n=n, src=src):
+            local(src, o_act.at[0, n], act_sem.at[n]).wait()
 
         @when(level == 3)
-        def _(n=n):
-            act_copy(acts.at[n], 0, n, 0, p.above).wait_recv()
+        def _(n=n, src=src):
+            act_copy(src, 0, n, 0, p.above).wait_recv()
 
         @when((level == 0) | (level == 3))
-        def _(n=n):
-            act_copy(acts.at[n], 1, n, 1, p.above).wait_recv()
-
-
-def run_reduce(grads, acts):
+        def _(n=n, src=src):
+            act_copy(src, 1, n, 1, p.above).wait_recv()
+
+    local(small, o_small.at[0], ct_sem.at[1]).wait()
+    local(small_in.at[5], o_small.at[1], ct_sem.at[2]).wait()
+
+
+SMALL = (LAYERS, 24, BLOCK)
+
+
+def run_backward(saved, vectors):
     dma = pltpu.SemaphoreType.DMA
     slots = dma((SLOTS,))
     units = dma((TOTAL,))
+    pair = dma((TOTAL, 2))
     return pl.pallas_call(
-        reduce_kernel,
+        backward_kernel,
         out_shape=(
             jax.ShapeDtypeStruct((TOTAL, 96, BLOCK), f32),
             jax.ShapeDtypeStruct((2, 3, ROWS, WIDTH), f32),
+            jax.ShapeDtypeStruct((2, *SMALL), f32),
         ),
-        in_specs=[ANY, ANY],
-        out_specs=(ANY, ANY),
+        in_specs=[ANY] * 12 + [VMEM],
+        out_specs=(ANY,) * 3,
         scratch_shapes=[
             pltpu.VMEM((SLOTS, 2, 2, 2, 2, 96, BLOCK), f32),
             pltpu.VMEM((SLOTS, 2, 2, 96, BLOCK), f32),
@@ -869,6 +1147,25 @@
             pltpu.VMEM((TOTAL, 2, 2, 96, BLOCK), f32),
             pltpu.VMEM((TOTAL, 2, 2, 96, BLOCK), f32),
             pltpu.VMEM((TOTAL, 2, 96, BLOCK), f32),
+            pltpu.VMEM((ROWS, WIDTH), f32),
+            pltpu.VMEM((ROWS, WIDTH), f32),
+            pltpu.VMEM((2, ROWS, WIDTH), f32),
+            pltpu.VMEM((ROWS, WIDTH), f32),
+            pltpu.VMEM((ROWS, WIDTH), f32),
+            pltpu.VMEM((ROWS, WIDTH), bf16),
+            pltpu.VMEM((ROWS, WIDTH), bf16),
+            pltpu.VMEM((2, ROWS, 192), bf16),
+            pltpu.VMEM((2, ROWS, 192), bf16),
+            pltpu.VMEM((2, ROWS, 192), bf16),
+            pltpu.VMEM((2, ROWS, 192), bf16),
+            pltpu.VMEM((2, 2, ROWS, BLOCK), f32),
+            pltpu.VMEM((2, 2, ROWS, BLOCK), bf16),
+            pltpu.VMEM((2, UNITS, WIDTH, BLOCK), bf16),
+            pltpu.VMEM((ROWS, WIDTH), bf16),
+            pltpu.VMEM((2, ROWS, BLOCK), bf16),
+            pltpu.VMEM((2, ROWS, 192), bf16),
+            pltpu.VMEM(SMALL, f32),
+            pltpu.VMEM((6, *SMALL), f32),
             slots,
             slots,
             slots,
@@ -877,9 +1174,8 @@
             slots,
             slots,
             slots,
-            slots,
-            dma((TOTAL, 2)),
-            dma((TOTAL, 2)),
+            pair,
+            pair,
             units,
             units,
             units,
@@ -888,96 +1184,18 @@
             dma((3, 3)),
             dma((3, 2)),
             dma((3,)),
+            dma((10,)),
+            dma((UNITS,)),
+            dma((4,)),
+            dma((6,)),
+            dma((6,)),
+            dma((3,)),
         ],
         compiler_params=pltpu.CompilerParams(
-            collective_id=1, has_side_effects=True, vmem_limit_bytes=60 << 20
+            collective_id=1, has_side_effects=True, vmem_limit_bytes=63 << 20
         ),
-        name="reduce_gradients",
-    )(grads, acts)
-
-
-def sum_cores(value):
-    size = lax.axis_size("dp")
-    return value + lax.ppermute(value, "dp", [(i, i + 1 - 2 * (i % 2)) for i in range(size)])
-
-
-def backward(saved, vectors):
-    x_in, cotangent, hs, ms, n1s, n2s, qs, ks, vs, as_, us, cs, low = saved
-    keep = lax.broadcasted_iota(jnp.int32, (ROWS, ROWS), 1) < FRAMES
-    upstream = cotangent
-    units = []
-    vector_grads = [None] * LAYERS
-    head_grads = [None] * LAYERS
-    up_grads = [None] * LAYERS
-    for l in reversed(range(LAYERS)):
-        params = vectors[l]
-        base = UNITS * l
-        scaled_two, inverse_two = normalize_parts(ms[l])
-        scaled_one, inverse_one = normalize_parts(x_in if l == 0 else hs[l - 1])
-        output_low = upstream.astype(bf16)
-        down_bias_grad = jnp.sum(output_low.astype(f32), axis=0)
-        for k in range(2):
-            units.append(jnp.stack([contract_rows(output_low, cs[l, j, k]) for j in range(2)]))
-        partial = 0.0
-        up_rows = [[None, None], [None, None]]
-        for k in range(2):
-            pair = []
-            for j in range(2):
-                back = (product(output_low, low[j, base + 4 + k]) * gelu_slope(us[l, j, k])).astype(bf16)
-                up_rows[j][k] = jnp.sum(back.astype(f32), axis=0)
-                pair.append(contract_rows(n2s[l], back))
-                partial = partial + contract_last(back, low[j, base + 2 + k])
-            units.append(jnp.stack(pair))
-        lowered, gain_two_grad, shift_two_grad = normalize_back(
-            sum_cores(partial), scaled_two, inverse_two, params[2]
-        )
-        upstream = upstream + lowered
-        branch_low = upstream.astype(bf16)
-        out_bias_grad = jnp.sum(branch_low.astype(f32), axis=0)
-        partial = 0.0
-        vo_units, qk_units, head_rows = [], [], []
-        for j in range(2):
-            w_out = low[j, base + 1][:, 192:]
-            out_grad = contract_rows(branch_low, as_[l, j])
-            mixture_back = product(branch_low, w_out).astype(bf16)
-            dq, dk, dv = [], [], []
-            for h in range(HEADS_HERE):
-                cols = slice(HEAD_DIM * h, HEAD_DIM * (h + 1))
-                q, k, v, da = qs[l, j][:, cols], ks[l, j][:, cols], vs[l, j][:, cols], mixture_back[:, cols]
-                scores = jnp.where(keep, contract_last(q, k) * score_scale, -1e30)
-                weight = jnp.exp(scores - jnp.max(scores, axis=-1, keepdims=True))
-                weight = weight * (1.0 / jnp.sum(weight, axis=-1, keepdims=True))
-                prob_grad = contract_last(da, v)
-                centre = jnp.sum(prob_grad * weight, axis=-1, keepdims=True)
-                score_back = (weight * (prob_grad - centre)).astype(bf16)
-                dq.append((product(score_back, k) * score_scale).astype(bf16))
-                dk.append((contract_rows(score_back, q) * score_scale).astype(bf16))
-                dv.append(contract_rows(weight.astype(bf16), da).astype(bf16))
-            dq, dk, dv = (jnp.concatenate(parts, axis=-1) for parts in (dq, dk, dv))
-            vo_units.append(jnp.concatenate([contract_rows(n1s[l], dv), out_grad], axis=-1))
-            qk_units.append(
-                jnp.concatenate([contract_rows(n1s[l], dq), contract_rows(n1s[l], dk)], axis=-1)
-            )
-            partial = (
-                partial
-                + contract_last(dq, low[j, base][:, :192])
-                + contract_last(dk, low[j, base][:, 192:])
-                + contract_last(dv, low[j, base + 1][:, :192])
-            )
-            head_rows.append((jnp.sum(dq.astype(f32), axis=0), jnp.sum(dv.astype(f32), axis=0)))
-        units.append(jnp.stack(vo_units))
-        units.append(jnp.stack(qk_units))
-        lowered, gain_one_grad, shift_one_grad = normalize_back(
-            sum_cores(partial), scaled_one, inverse_one, params[0]
-        )
-        upstream = upstream + lowered
-        vector_grads[l] = jnp.stack(
-            [gain_one_grad, shift_one_grad, gain_two_grad, shift_two_grad, out_bias_grad, down_bias_grad]
-        )
-        head_grads[l] = jnp.stack([jnp.stack([head_rows[j][n] for n in range(2)]) for j in range(2)])
-        up_grads[l] = jnp.stack([jnp.concatenate(up_rows[j]) for j in range(2)])
-    grads = jnp.stack(units).reshape(TOTAL, 2, 2, 2, 2, 96, BLOCK)
-    return upstream, grads, jnp.stack(vector_grads), jnp.stack(head_grads), jnp.stack(up_grads)
+        name="backward_reduce",
+    )(*saved, vectors)
 
 
 def per_device(
@@ -1021,34 +1239,26 @@
     bias = jnp.pad(bias, ((0, 8 - 3 * LAYERS), (0, 0)))
     saved = run_forward(clips_of(frames), clips_of(cotangent), wa, wm, bias, vectors)
 
-    input_grad, grads, vector_grad, head_grad, up_grad = backward(saved, vectors)
-
-    acts = jnp.concatenate([saved[2], input_grad[None]])
-    fin, acts = run_reduce(grads, acts)
+    fin, acts, small = run_backward(saved, vectors)
 
     acts = acts[:, :, :FRAMES]
     acts = jnp.where(core == 0, acts, acts[::-1])
     acts = jnp.concatenate([acts[0], acts[1]], axis=1)
     sections, upstream = acts[:2], acts[2]
 
-    def in_order(pair, axis):
-        return jnp.where(core == 0, pair, jnp.flip(pair, axis))
-
-    head_grad = in_order(head_grad, 1).transpose(0, 2, 1, 3).reshape(LAYERS, 2, 2 * HEADS_HERE, HEAD_DIM)
-    up_grad = in_order(up_grad, 1).reshape(LAYERS, 24, HEAD_DIM)
-    head_all = jnp.concatenate(
-        [jnp.where(core == k, head_grad, 0.0) for k in range(2)], axis=2
-    )
-    up_all = jnp.concatenate([jnp.where(core == k, up_grad, 0.0) for k in range(2)], axis=1)
-    vector_all = jnp.where(core == 0, vector_grad, 0.0)
-    vector_all, head_all, up_all = lax.psum((vector_all, head_all, up_all), ("dp", "tensor"))
+    if dp_size > GROUP:
+        groups = [[i + GROUP * o for o in range(dp_size // GROUP)] for i in range(GROUP)]
+        small = lax.psum(small, "dp", axis_index_groups=groups)
+    vector_all = small[0, :, :12].reshape(LAYERS, 6, WIDTH)
+    owner = t // 2
+    here = jnp.where(owner == core, small[0], small[1])
+    second = jnp.where(owner == 0, t % 2, 1 - t % 2)
+    head_all = jnp.where(second == 0, here[:, 12], here[:, 13]).reshape(LAYERS, 2, HEADS_HERE, HEAD_DIM)
+    up_all = jnp.where(second == 0, here[:, 14:16], here[:, 16:18]).reshape(LAYERS, 12, HEAD_DIM)
 
     def owned(param, dim):
         size = param.shape[dim] // dp_size
         return lax.dynamic_slice_in_dim(param, dp * size, size, dim)
-
-    head_all = lax.dynamic_slice_in_dim(head_all, t * HEADS_HERE, HEADS_HERE, 2)
-    up_all = lax.dynamic_slice_in_dim(up_all, t * 12, 12, 1)
 
     if dp_size > GROUP:
         rows = jnp.zeros((TOTAL, WIDTH, BLOCK), f32)

time: 952 us -> 649 us (0.68)
  matrix products: 135 us -> 0 us
  waiting for transfers between devices: 108 us -> 0 us
  Pallas kernels: 475 us -> 570 us
  other arithmetic: 101 us -> 26 us
  local copies, waits for them, and re-layouts: 107 us -> 41.2 us
  between operations: 16.4 us -> 1.38 us
    dot_general x124 -> x0, matrix products: 135 us -> none  [the longest x56 58.1 us: contract_rows(): lax.dot_general(left, right, (((0,), (0,)), ((), ())), preferred_element_...]
    psum x1 -> x0, waiting for transfers between devices: 108 us -> none  [per_device(): lax.psum((vector_all, head_all, up_all), ('dp', 'tensor'))]
    pallas_call x2, Pallas kernels: 475 us -> 570 us  [the longest x1 355 us: run_backward(): pl.pallas_call(backward_kernel, out_shape=(jax.ShapeDtypeStruct((TOTAL, 9...]
    reduce_sum x34 -> x0, other arithmetic: 31 us -> none  [the longest x4 12.8 us: normalize_back(): gain_grad = jnp.sum(upstream * scaled, axis=0)]
    unnamed x371 -> x48, local copies, waits for them, and re-layouts: 30.9 us -> 7.06 us
    unnamed x11 -> x0, other arithmetic: 22.9 us -> none
    concatenate x8 -> x0, local copies, waits for them, and re-layouts: 18.9 us -> none  [the longest x4 9.45 us: backward(): jnp.concatenate([contract_rows(n1s[l], dq), contract_rows(n1s[l], dk)], a...]
    concatenate x15 -> x0, other arithmetic: 11.8 us -> none  [the longest x4 4.59 us: backward(): jnp.concatenate([contract_rows(n1s[l], dv), out_grad], axis=-1)]
  transfers between devices with their start and end apart: 5 -> 0, of which waited for: 1 -> 0; matrix products, arithmetic and copies ran while one was open for 16% -> 0% of each run, Pallas kernels for 0% -> 0%
where the time goes in v2:
time: 649 us; the launch traced here: 639 us
  Pallas kernels  570 us (88%)
  local copies, waits for them, and re-layouts  41.2 us (6%)
  other arithmetic  26 us (4%)
    pallas_call x1, Pallas kernels, run_backward(): pl.pallas_call(backward_kernel, out_shape=(jax.ShapeDtypeStruct((TOTAL, 9...  355 us
    pallas_call x1, Pallas kernels, run_forward(): pl.pallas_call(forward_kernel, out_shape=(hbm((ROWS, WIDTH), f32), hbm((L...  216 us

profile of v2, /device:TPU:0, one launch (start us, length us, event | category | flops | bytes accessed | tf_op | source)
XLA Modules:
  0.0 639.0 jit_solution(5194919844475210333)
XLA Ops:
  0.7 4.2 fusion.17
  5.3 1.7 copy.74
  7.1 2.9 copy.75
  10.0 2.9 copy.76
  12.9 5.1 maximum_maximum_fusion.wa
  18.0 0.6 copy.80.vec
  19.4 2.2 reshape.75
  21.6 1.8 pad.11.frames
  23.4 2.2 reshape.76
  25.6 1.8 pad.12.cotangent
  27.4 215.7 %gather_forward.1 = (f32[512,768]{1,0:T(8,128)}, f32[3,512,768]{2,1,0:T(8,128)}, f32[2,512,768]{2,1,0:T(8,128)}, bf16[2,512,768]{2,1,0:T(8,128)(2,1)}, bf16[2,51...) custom-call(f32[2,512,768]{2,1,0:T(8,128)} %pad.11.frames, ...), custom_call_target="tpu_custom_call" | custom-call | tf_op jit(solution)/shard_map/gather_forward/pallas_call | solution.py:556
  243.1 354.6 %backward_reduce.1 = (f32[12,96,384]{2,1,0:T(8,128)}, f32[2,3,512,768]{3,2,1,0:T(8,128)}, f32[2,2,24,384]{3,2,1,0:T(8,128)}) custom-call(f32[512,768]{1,0:T(8,128)} %get-tuple-element.32.i_ct, f32[3,512,768]{2,1,0:T(8,128)} %get-tuple-element.33.i_h, f32[2,512,768]{2,1,0:T(8,128)} %get-tuple-element.34.i_m, bf16[2,512,768]{2,1,0:T(8,128)(2,1)} %get-tuple-element.35.i_n1, ...), custom_call_target="tpu_custom_call" | custom-call | tf_op jit(solution)/shard_map/backward_reduce/pallas_call | solution.py:1132
  597.8 2.4 slice_bitcast_fusion.9
  600.4 1.1 copy-done
  601.9 3.7 multiply_subtract_fusion
  605.7 0.7 copy-done.2
  606.7 1.8 constant_dynamic-slice_fusion.2
  608.8 2.9 multiply_subtract_fusion.1
  611.7 7.8 %slice.116 = f32[2,3,500,768]{3,2,1,0:T(8,128)} slice(f32[2,3,512,768]{3,2,1,0:T(8,128)} %get-tuple-element.44), slice={[0:2], [0:3], [0:500], [0:768]} | slice | bytes 18432000 | tf_op jit(solution)/shard_map/slice | solution.py:1244
  619.5 7.6 %reverse_select_fusion = f32[2,3,500,768]{3,2,1,0:T(8,128)S(1)} fusion(f32[2,3,500,768]{3,2,1,0:T(8,128)} %slice.116, pred[]{:T(512)S(6)} %eq.17), kind=kLoop, calls=%fused_computation | loop fusion | flops 2304000 | bytes 18432000 | tf_op jit(solution)/shard_map/jit(_where)/select_n | solution.py:1245
  627.7 1.9 fusion.1
  629.7 3.1 fusion
  633.2 0.6 multiply_subtract_fusion.2
  635.9 0.8 multiply_subtract_fusion.4
  (70 shorter events, 7.4 us)
Async XLA Ops:
  12.9 5.1 copy-start.10
  12.9 5.7 copy-start.13
  12.9 5.8 copy-start.8
  600.2 1.3 copy-start
  600.2 1.6 copy-start.1
  601.9 3.7 copy-start.4
  601.9 3.7 copy-start.5
  605.5 0.9 copy-start.2
  605.5 1.0 copy-start.3
  606.7 2.1 copy-start.6
  629.6 3.1 copy-start.7
  629.6 3.4 copy-start.9
  629.6 3.6 copy-start.11
  629.6 3.6 copy-start.12
  629.6 4.3 copy-start.14
  629.6 4.3 copy-start.15
  629.6 6.2 copy-start.16
  629.6 6.2 copy-start.17

commit v3 on v2

v3 whole, which is shorter than its diff:
```python
import math
from types import SimpleNamespace

import jax
import jax.numpy as jnp
from jax import lax
from jax.experimental import pallas as pl
from jax.experimental.pallas import tpu as pltpu
from jax.sharding import PartitionSpec as P

HEAD_DIM = 64
FRAMES = 500
ROWS = 512
LAYERS = 2
STEP = 10
WIDTH = 768
BLOCK = 384
UNITS = 6
TOTAL = LAYERS * UNITS
GROUP = 8
HEADS_HERE = 3
SLOTS = 3
SPAN = 504
SECOND = 496
CHUNK = 128

ln_eps = 1e-05
beta_one = 0.9
beta_two = 0.999
adam_eps = 1e-08
decay_rate = 0.01
rate_matrix = 0.05
rate_vector = 0.2
score_scale = 1.0 / math.sqrt(HEAD_DIM)
MESH = pl.DeviceIdType.MESH
f32 = jnp.float32
bf16 = jnp.bfloat16
ANY = pl.BlockSpec(memory_space=pl.ANY)
VMEM = pl.BlockSpec(memory_space=pltpu.VMEM)


def product(left, right):
    return jnp.dot(left, right, preferred_element_type=f32)


def contract_last(left, right):
    return lax.dot_general(left, right, (((1,), (1,)), ((), ())), preferred_element_type=f32)


def contract_rows(left, right):
    return lax.dot_general(left, right, (((0,), (0,)), ((), ())), preferred_element_type=f32)


def normalize_parts(inputs):
    centre = jnp.mean(inputs, axis=-1, keepdims=True)
    centred = inputs - centre
    inverse = lax.rsqrt(jnp.mean(centred * centred, axis=-1, keepdims=True) + ln_eps)
    return centred * inverse, inverse


def normalize_back(upstream, scaled, inverse, gain):
    gain_grad = jnp.sum(upstream * scaled, axis=0)
    shift_grad = jnp.sum(upstream, axis=0)
    inner_grad = upstream * gain
    lowered = inverse * (
        inner_grad
        - jnp.mean(inner_grad, axis=-1, keepdims=True)
        - scaled * jnp.mean(inner_grad * scaled, axis=-1, keepdims=True)
    )
    return (lowered, gain_grad, shift_grad)


def gelu(before):
    return 0.5 * before * (1.0 + lax.erf(before * (1.0 / math.sqrt(2.0))))


def gelu_slope(before):
    return 0.5 * (1.0 + lax.erf(before * (1.0 / math.sqrt(2.0)))) + before * jnp.exp(
        -0.5 * before * before
    ) * (1.0 / math.sqrt(2.0 * math.pi))


def adamw_update(param, gradient, first, second, rate):
    first_new = beta_one * first + (1.0 - beta_one) * gradient
    second_new = beta_two * second + (1.0 - beta_two) * gradient * gradient
    ratio = (
        first_new
        / (1.0 - beta_one**STEP)
        / (jnp.sqrt(second_new / (1.0 - beta_two**STEP)) + adam_eps)
    )
    return (param - rate * (ratio + decay_rate * param), first_new, second_new)


def find_place():
    dp = lax.axis_index("dp")
    t = lax.axis_index("tensor")
    i = lax.rem(dp, GROUP)
    base = dp - i
    c = lax.rem(i, 2)
    x = lax.rem(i // 2, 2)
    y = i // 4
    up = 1 - 2 * c
    level = c * (3 - t) + (1 - c) * t

    def at(cc, xx, yy):
        return base + 4 * yy + 2 * xx + cc

    return SimpleNamespace(
        t=t,
        c=c,
        x=x,
        y=y,
        q=2 * y + x,
        qx=2 * y + 1 - x,
        qy=2 * (1 - y) + x,
        qd=2 * (1 - y) + 1 - x,
        level=level,
        partner=(at(1 - c, x, y), t),
        xn=(at(c, 1 - x, y), t),
        yn=(at(c, x, 1 - y), t),
        above=(dp, t + up),
        below=(dp, t - up),
    )


def greet(p):
    barrier = pltpu.get_barrier_semaphore()

    def signal(device):
        pl.semaphore_signal(barrier, inc=1, device_id=device, device_id_type=MESH)

    signal(p.partner)
    signal(p.xn)
    signal(p.yn)

    @pl.when(p.level < 3)
    def _():
        signal(p.above)

    @pl.when(p.level > 0)
    def _():
        signal(p.below)

    inner = (p.level > 0) & (p.level < 3)

    @pl.when(inner)
    def _():
        pl.semaphore_wait(barrier, 5)

    @pl.when(jnp.logical_not(inner))
    def _():
        pl.semaphore_wait(barrier, 4)


def remote(src, dst, send_sem, recv_sem, device):
    return pltpu.make_async_remote_copy(
        src_ref=src,
        dst_ref=dst,
        send_sem=send_sem,
        recv_sem=recv_sem,
        device_id=device,
        device_id_type=MESH,
    )


def local(src, dst, sem):
    return pltpu.make_async_copy(src, dst, sem)


def forward_kernel(
    frames,
    cotangent,
    wa,
    wm,
    head_bias,
    up_bias,
    vec,
    o_ct,
    o_h,
    o_m,
    o_n1,
    o_n2,
    o_qk,
    o_v,
    o_a,
    o_u,
    o_c,
    o_wa,
    o_wm,
    ga,
    gm,
    hb,
    ub,
    hs,
    ms,
    n1s,
    n2s,
    qks,
    vs,
    as_,
    us,
    cs,
    low_a,
    low_m,
    part,
    other,
    rz,
    sz,
    szd,
    rx,
    sx,
    ry,
    sy,
    rxd,
    sxd,
    ryd,
    syd,
    native,
    first_sem,
    bias_local,
    bias_send,
    bias_recv,
    swap_sem,
    low_sem,
    mid_sem,
    out_sem,
):
    p = find_place()
    greet(p)
    level = p.level
    when = pl.when

    def quarter(ref, i, q, h=None):
        lead = (slice(None), q) if i < 2 else (q,)
        return ref.at[lead if h is None else (*lead, h)]

    def block(l, i):
        if i < 2:
            return wa.at[l, pl.ds(2 * i, 2)]
        return wm.at[l, (i - 2) // 2, :, :, :, pl.ds(BLOCK * (i % 2), BLOCK)]

    def block_quarter(l, i):
        if i < 2:
            return wa.at[l, pl.ds(2 * i, 2), p.q]
        return wm.at[l, (i - 2) // 2, p.q, :, :, pl.ds(BLOCK * (i % 2), BLOCK)]

    def held(l, i, j):
        return ga.at[j, l, i] if i < 2 else gm.at[j, l, i - 2]

    def z_copy(src, l, i, j, device, send_sem):
        return remote(src, quarter(held(l, i, j), i, p.q), send_sem, rz.at[UNITS * l + i, j], device)

    def plane_copy(l, i, j, q, h, send_sem, recv_sem, device):
        here = quarter(held(l, i, j), i, q, h)
        u = UNITS * l + i
        return remote(here, here, send_sem.at[u, j], recv_sem.at[u, j], device)

    def x_copy(l, i, j, q):
        return plane_copy(l, i, j, q, None, sx, rx, p.xn)

    def y_copy(l, i, j, q):
        return plane_copy(l, i, j, q, None, sy, ry, p.yn)

    def xd_copy(l, i, j, q):
        return plane_copy(l, i, j, q, 1, sxd, rxd, p.xn)

    def yd_copy(l, i, j, q):
        return plane_copy(l, i, j, q, 0, syd, ryd, p.yn)

    def source(l, i):
        u = UNITS * l + i

        @when(level == 0)
        def _():
            z_copy(block_quarter(l, i), l, i, 0, p.above, sz.at[u, 0]).start()
            local(block(l, i), held(l, i, 0), native.at[u]).start()

        @when(level == 1)
        def _():
            z_copy(block_quarter(l, i), l, i, 1, p.above, sz.at[u, 1]).start()
            z_copy(block_quarter(l, i), l, i, 1, p.below, szd.at[u]).start()
            local(block(l, i), held(l, i, 1), native.at[u]).start()

    def stage_one(l, i):
        u = UNITS * l + i
        for j in range(2):

            @when(level != j)
            def _(j=j):
                here = quarter(held(l, i, j), i, p.q)
                z_copy(here, l, i, j, p.above, sz.at[u, j]).wait_recv()

                @when((level == 2) | ((level == 1) if j == 0 else (level == 2)))
                def _():
                    z_copy(here, l, i, j, p.above, sz.at[u, j]).start()

                x_copy(l, i, j, p.q).start()
                y_copy(l, i, j, p.q).start()

    def stage_two(l, i):
        for j in range(2):

            @when(level != j)
            def _(j=j):
                x_copy(l, i, j, p.qx).wait_recv()
                yd_copy(l, i, j, p.qx).start()
                y_copy(l, i, j, p.qy).wait_recv()
                xd_copy(l, i, j, p.qy).start()

    def finish(l, i):
        u = UNITS * l + i
        for j in range(2):

            @when(level != j)
            def _(j=j):
                yd_copy(l, i, j, p.qd).wait_recv()
                xd_copy(l, i, j, p.qd).wait_recv()

            @when(level == j)
            def _(j=j):
                local(block(l, i), held(l, i, j), native.at[u]).wait()

    def ahead(step, l, i, by):
        k = i + by
        if k < UNITS:
            step(l, k)
        else:

            @when(l + k // UNITS < LAYERS)
            def _():
                step(l + k // UNITS, k % UNITS)

    def tick(l, i):
        ahead(source, l, i, 3)
        ahead(stage_one, l, i, 2)
        ahead(stage_two, l, i, 1)
        finish(l, i)

    mine = (p.t // 2) == p.c
    clip = lax.rem(p.t, 2)
    span = pl.ds(pl.multiple_of(clip * SECOND, 8), SPAN)
    inputs = (
        (frames.at[span], part.at[pl.ds(0, SPAN)]),
        (cotangent.at[span], ms.at[1, pl.ds(0, SPAN)]),
    )

    def input_copies(k):
        src, dst = inputs[k]
        return (
            local(src, dst, first_sem.at[k]),
            remote(src, dst, first_sem.at[2 + k], first_sem.at[4 + k], p.partner),
        )

    def wait_input(k):
        here, there = input_copies(k)

        @when(mine)
        def _():
            here.wait()
            there.wait_send()

        @when(jnp.logical_not(mine))
        def _():
            there.wait_recv()

    def take_clip(target, raw):
        @when(clip == 0)
        def _():
            target[0:FRAMES] = raw[0:FRAMES]

        @when(clip == 1)
        def _():
            target[0:FRAMES] = raw[FRAMES - SECOND : SPAN]

        target[FRAMES:ROWS] = jnp.zeros((ROWS - FRAMES, WIDTH), f32)

    kept_biases = ((head_bias, hb), (up_bias, ub))

    def bias_copy(src, n, j, m, device):
        return remote(src, kept_biases[n][1].at[j], bias_send.at[n, m], bias_recv.at[n, j], device)

    def bias_source():
        for n, (src, dst) in enumerate(kept_biases):

            @when(level == 0)
            def _(n=n, src=src, dst=dst):
                local(src, dst.at[0], bias_local.at[n]).start()
                bias_copy(src, n, 0, 0, p.above).start()

            @when(level == 1)
            def _(n=n, src=src, dst=dst):
                local(src, dst.at[1], bias_local.at[n]).start()
                bias_copy(src, n, 1, 1, p.above).start()
                bias_copy(src, n, 1, 2, p.below).start()

    def bias_pass():
        for n, (src, dst) in enumerate(kept_biases):

            @when(level != 0)
            def _(n=n, src=src):
                bias_copy(src, n, 0, 0, p.above).wait_recv()

            @when((level == 1) | (level == 2))
            def _(n=n, dst=dst):
                bias_copy(dst.at[0], n, 0, 0, p.above).start()

            @when(level != 1)
            def _(n=n, src=src):
                bias_copy(src, n, 1, 1, p.above).wait_recv()

            @when(level == 2)
            def _(n=n, dst=dst):
                bias_copy(dst.at[1], n, 1, 1, p.above).start()

            @when(level < 2)
            def _(n=n, src=src, dst=dst):
                local(src, dst.at[0], bias_local.at[n]).wait()

    def bias_drain():
        for n, (src, dst) in enumerate(kept_biases):

            @when(level < 3)
            def _(n=n, src=src):
                bias_copy(src, n, 0, 0, p.above).wait_send()

            @when((level == 1) | (level == 2))
            def _(n=n, src=src):
                bias_copy(src, n, 1, 1, p.above).wait_send()

            @when(level == 1)
            def _(n=n, src=src):
                bias_copy(src, n, 1, 2, p.below).wait_send()

    def row_of(ref, rows):
        return jnp.concatenate([ref[r : r + 1, :] for r in rows], axis=-1)

    @when(mine)
    def _():
        for copy in input_copies(0):
            copy.start()

    bias_source()
    for i in range(3):
        source(0, i)

    @when(mine)
    def _():
        for copy in input_copies(1):
            copy.start()

    bias_pass()
    stage_one(0, 0)
    wait_input(0)
    take_clip(hs.at[0], part)
    stage_one(0, 1)
    stage_two(0, 0)
    wait_input(1)
    take_clip(part, ms.at[1])
    keep_cotangent = local(part, o_ct, out_sem.at[0, 1])
    keep_cotangent.start()
    keep_cotangent.wait()

    def keep_low(l, i):
        if i < 2:
            slots, slot, target = low_a, 0, lambda j: o_wa.at[j, l, i]
        else:
            slots, slot, target = low_m, i % 2, lambda j: o_wm.at[j, l, i - 2]
        sems = 0 if i < 2 else 1 + i % 2

        def copy(j):
            return local(slots.at[slot, j], target(j), low_sem.at[sems, j])

        def drain():
            for j in range(2):
                copy(j).wait()

        if i in (1, 4, 5):
            drain()
        else:
            when(l > 0)(drain)
        for j in range(2):
            if i < 2:
                slots[slot, j] = ga[j, l, i].reshape(BLOCK, WIDTH).astype(bf16)
            else:
                slots[slot, j] = gm[j, l, i - 2].reshape(WIDTH, BLOCK).astype(bf16)
            copy(j).start()
        return slots.at[slot]

    def swap(slot):
        copy = remote(part, other.at[slot], swap_sem.at[slot], swap_sem.at[2 + slot], p.partner)
        copy.start()
        copy.wait()

    def out_copies(l):
        return [
            local(hs.at[l], o_h.at[l], out_sem.at[0, l]),
            local(ms.at[l], o_m.at[l], out_sem.at[1, l]),
            local(n1s.at[l], o_n1.at[l], out_sem.at[2, l]),
            local(n2s.at[l], o_n2.at[l], out_sem.at[3, l]),
            local(qks.at[l], o_qk.at[l], out_sem.at[4, l]),
            local(vs.at[l], o_v.at[l], out_sem.at[5, l]),
            local(as_.at[l], o_a.at[l], out_sem.at[6, l]),
        ]

    def mid_copies(l, i):
        k = i - 2
        return [
            local(us.at[:, k], o_u.at[l, :, k], mid_sem.at[0, k]),
            local(cs.at[:, k], o_c.at[l, :, k], mid_sem.at[1, k]),
        ]

    def layer(l, carry):
        params = vec[l]

        tick(l, 0)
        scaled, _ = normalize_parts(hs[l])
        n1s[l] = (scaled * params[0:1] + params[1:2]).astype(bf16)
        weights = keep_low(l, 0)
        for j in range(2):
            both = contract_last(n1s[l], weights[j])
            shift = jnp.concatenate([row_of(hb.at[j, l, 0], range(HEADS_HERE)), jnp.zeros((1, 192), f32)], axis=-1)
            qks[l, j] = (both + shift).astype(bf16)

        tick(l, 1)
        weights = keep_low(l, 1)
        keep = lax.broadcasted_iota(jnp.int32, (128, ROWS), 1) < FRAMES
        for j in range(2):
            vs[l, j] = (
                contract_last(n1s[l], weights[j, 0:192]) + row_of(hb.at[j, l, 1], range(HEADS_HERE))
            ).astype(bf16)

            def rows_of(r, carry, j=j):
                rows = pl.ds(pl.multiple_of(r * 128, 128), 128)
                heads = []
                for h in range(HEADS_HERE):
                    cols = slice(HEAD_DIM * h, HEAD_DIM * (h + 1))
                    k_cols = slice(192 + HEAD_DIM * h, 192 + HEAD_DIM * (h + 1))
                    scores = contract_last(qks[l, j, rows, cols], qks[l, j, :, k_cols]) * score_scale
                    scores = jnp.where(keep, scores, -1e30)
                    weight = jnp.exp(scores - jnp.max(scores, axis=-1, keepdims=True))
                    weight = weight * (1.0 / jnp.sum(weight, axis=-1, keepdims=True))
                    heads.append(product(weight.astype(bf16), vs[l, j, :, cols]))
                as_[l, j, rows, :] = jnp.concatenate(heads, axis=-1).astype(bf16)
                return carry

            lax.fori_loop(0, ROWS // 128, rows_of, 0)
        part[...] = product(as_[l, 0], weights[0, 192:384])
        part[...] += product(as_[l, 1], weights[1, 192:384])
        swap(0)
        ms[l] = hs[l] + (part[...] + other[0]) + params[4:5]
        scaled, _ = normalize_parts(ms[l])
        n2s[l] = (scaled * params[2:3] + params[3:4]).astype(bf16)
        for copy in out_copies(l):
            copy.start()

        for i in (2, 3):
            tick(l, i)
            weights = keep_low(l, i)

            @when(l > 0)
            def _(i=i):
                for copy in mid_copies(l - 1, i):
                    copy.wait()

            for j in range(2):
                shift = row_of(ub.at[j, l], range(6 * (i - 2), 6 * (i - 1)))
                before = product(n2s[l], weights[j]) + shift
                us[j, i - 2] = before
                cs[j, i - 2] = gelu(before).astype(bf16)
            for copy in mid_copies(l, i):
                copy.start()

        for i in (4, 5):
            tick(l, i)
            weights = keep_low(l, i)

            @when(l < LAYERS - 1)
            def _(i=i, weights=weights):
                for j in range(2):
                    term = contract_last(cs[j, i - 4], weights[j])
                    if i == 4 and j == 0:
                        part[...] = term
                    else:
                        part[...] += term

        @when(l < LAYERS - 1)
        def _():
            swap(1)
            hs[l + 1] = ms[l] + (part[...] + other[1]) + params[5:6]

        return carry

    lax.fori_loop(0, LAYERS, layer, 0)

    last = LAYERS - 1
    for i in (2, 3):
        for copy in mid_copies(last, i):
            copy.wait()
    for l in range(LAYERS):
        for copy in out_copies(l):
            copy.wait()
    for j in range(2):
        local(low_a.at[0, j], o_wa.at[j, last, 1], low_sem.at[0, j]).wait()
        for slot in range(2):
            local(low_m.at[slot, j], o_wm.at[j, last, 2 + slot], low_sem.at[1 + slot, j]).wait()
    bias_drain()

    def drain(u, carry):
        l = u // UNITS
        for j in range(2):

            @when((level < 3) if j == 0 else ((level == 1) | (level == 2)))
            def _(j=j):
                z_copy(gm.at[j, l, 0, p.q], l, 2, j, p.above, sz.at[u, j]).wait_send()

            @when(level != j)
            def _(j=j):
                whole, half = gm.at[j, l, 0, p.q], gm.at[j, l, 0, p.q, 0]
                remote(whole, whole, sx.at[u, j], rx.at[u, j], p.xn).wait_send()
                remote(whole, whole, sy.at[u, j], ry.at[u, j], p.yn).wait_send()
                remote(half, half, sxd.at[u, j], rxd.at[u, j], p.xn).wait_send()
                remote(half, half, syd.at[u, j], ryd.at[u, j], p.yn).wait_send()

        @when(level == 1)
        def _():
            z_copy(gm.at[1, l, 0, p.q], l, 2, 1, p.below, szd.at[u]).wait_send()

        return carry

    lax.fori_loop(0, TOTAL, drain, 0)


def run_forward(frames, cotangent, wa, wm, head_bias, up_bias, vectors):
    def hbm(shape, kind):
        return jax.ShapeDtypeStruct(shape, kind)

    dma = pltpu.SemaphoreType.DMA
    per_unit = dma((TOTAL, 2))
    return pl.pallas_call(
        forward_kernel,
        out_shape=(
            hbm((ROWS, WIDTH), f32),
            hbm((LAYERS, ROWS, WIDTH), f32),
            hbm((LAYERS, ROWS, WIDTH), f32),
            hbm((LAYERS, ROWS, WIDTH), bf16),
            hbm((LAYERS, ROWS, WIDTH), bf16),
            hbm((LAYERS, 2, ROWS, BLOCK), bf16),
            hbm((LAYERS, 2, ROWS, 192), bf16),
            hbm((LAYERS, 2, ROWS, 192), bf16),
            hbm((LAYERS, 2, 2, ROWS, BLOCK), f32),
            hbm((LAYERS, 2, 2, ROWS, BLOCK), bf16),
            hbm((2, LAYERS, 2, BLOCK, WIDTH), bf16),
            hbm((2, LAYERS, 4, WIDTH, BLOCK), bf16),
        ),
        in_specs=[ANY, ANY, ANY, ANY, ANY, ANY, VMEM],
        out_specs=(ANY,) * 12,
        scratch_shapes=[
            pltpu.VMEM((2, LAYERS, 2, 2, 4, 2, 24, WIDTH), f32),
            pltpu.VMEM((2, LAYERS, 4, 4, 2, 96, BLOCK), f32),
            pltpu.VMEM((2, *head_bias.shape), f32),
            pltpu.VMEM((2, *up_bias.shape), f32),
            pltpu.VMEM((LAYERS, ROWS, WIDTH), f32),
            pltpu.VMEM((LAYERS, ROWS, WIDTH), f32),
            pltpu.VMEM((LAYERS, ROWS, WIDTH), bf16),
            pltpu.VMEM((LAYERS, ROWS, WIDTH), bf16),
            pltpu.VMEM((LAYERS, 2, ROWS, BLOCK), bf16),
            pltpu.VMEM((LAYERS, 2, ROWS, 192), bf16),
            pltpu.VMEM((LAYERS, 2, ROWS, 192), bf16),
            pltpu.VMEM((2, 2, ROWS, BLOCK), f32),
            pltpu.VMEM((2, 2, ROWS, BLOCK), bf16),
            pltpu.VMEM((1, 2, BLOCK, WIDTH), bf16),
            pltpu.VMEM((2, 2, WIDTH, BLOCK), bf16),
            pltpu.VMEM((ROWS, WIDTH), f32),
            pltpu.VMEM((2, ROWS, WIDTH), f32),
            per_unit,
            per_unit,
            dma((TOTAL,)),
            per_unit,
            per_unit,
            per_unit,
            per_unit,
            per_unit,
            per_unit,
            per_unit,
            per_unit,
            dma((TOTAL,)),
            dma((6,)),
            dma((2,)),
            dma((2, 3)),
            dma((2, 2)),
            dma((4,)),
            dma((3, 2)),
            dma((2, 2)),
            dma((7, LAYERS)),
        ],
        compiler_params=pltpu.CompilerParams(
            collective_id=0, has_side_effects=True, vmem_limit_bytes=63 << 20
        ),
        name="gather_forward",
    )(frames, cotangent, wa, wm, head_bias, up_bias, vectors)


def backward_kernel(
    i_ct,
    i_h,
    i_m,
    i_n1,
    i_n2,
    i_qk,
    i_v,
    i_a,
    i_u,
    i_c,
    i_wa,
    i_wm,
    vec,
    o_fin,
    o_act,
    o_small,
    o_src,
    o_grads,
    held,
    x1,
    y1,
    x2,
    y2,
    own,
    zin,
    zup,
    stage,
    grad,
    part,
    other,
    h_in,
    m_in,
    n1,
    n2,
    qk,
    v,
    a,
    u_in,
    c_in,
    wa,
    wm,
    low,
    dqk,
    dv,
    small,
    small_in,
    sx1,
    rx1,
    sy1,
    ry1,
    sx2,
    rx2,
    sy2,
    ry2,
    szd,
    rzd,
    szu,
    rzu,
    sfin,
    rfin,
    lfin,
    act_send,
    act_recv,
    act_sem,
    load_sem,
    unit_sem,
    stage_sem,
    held_sem,
    swap_sem,
    small_send,
    small_recv,
    once_sem,
):
    p = find_place()
    greet(p)
    level = p.level
    when = pl.when

    chunks = ROWS // CHUNK
    n_chunks = 3 * chunks
    slot_of = (p.c, 1 - p.c)

    def act_part(ref, k):
        return ref.at[pl.ds(pl.multiple_of(lax.rem(k, chunks) * CHUNK, CHUNK), CHUNK)]

    def act_own(k):
        return act_part(o_src.at[k // chunks - 1], k)

    def act_there(j, k):
        return act_part(o_act.at[k // chunks, slot_of[j]], k)

    def act_copy(src, j, k, m, device):
        return remote(src, act_there(j, k), act_send.at[k, m], act_recv.at[k, j], device)

    def act_step(s):
        def between(k):
            return (k >= 0) & (k < n_chunks)

        def set_out(src):
            @when(level == 0)
            def _():
                act_copy(src, 0, s, 0, p.above).start()

            @when(level == 1)
            def _():
                act_copy(src, 1, s, 1, p.above).start()
                act_copy(src, 1, s, 2, p.below).start()

        when(between(s) & (s < chunks))(lambda: set_out(act_part(i_h.at[1], s)))
        when(between(s) & (s >= chunks))(lambda: set_out(act_own(s)))

        @when(between(s - 1) & (level == 1))
        def _():
            k = s - 1
            act_copy(act_there(0, k), 0, k, 0, p.above).wait_recv()
            act_copy(act_there(0, k), 0, k, 0, p.above).start()

        @when(between(s - 2) & (level == 2))
        def _():
            k = s - 2
            for j in (1, 0):
                act_copy(act_there(j, k), j, k, j, p.above).wait_recv()
                act_copy(act_there(j, k), j, k, j, p.above).start()

    def act_drain(k):
        @when(level < 3)
        def _():
            act_copy(act_there(0, k), 0, k, 0, p.above).wait_send()

        @when((level == 1) | (level == 2))
        def _():
            act_copy(act_there(1, k), 1, k, 1, p.above).wait_send()

        @when(level == 1)
        def _():
            act_copy(act_there(1, k), 1, k, 2, p.below).wait_send()

        @when(level == 3)
        def _():
            act_copy(act_there(0, k), 0, k, 0, p.above).wait_recv()

        @when((level == 0) | (level == 3))
        def _():
            act_copy(act_there(1, k), 1, k, 1, p.above).wait_recv()

    def act_local(src, n, method):
        for j in range(2):

            @when(level == j)
            def _(j=j):
                getattr(local(src, o_act.at[n, slot_of[j]], act_sem.at[n]), method)()

    def x1_copy(w):
        return remote(held.at[w, :, :, 1 - p.x, 0], x1.at[w], sx1.at[w], rx1.at[w], p.xn)

    def y1_copy(w):
        return remote(held.at[w, :, 1 - p.y, :, 1], y1.at[w], sy1.at[w], ry1.at[w], p.yn)

    def x2_copy(w):
        return remote(held.at[w, :, p.y, 1 - p.x, 1], x2.at[w], sx2.at[w], rx2.at[w], p.xn)

    def y2_copy(w):
        return remote(held.at[w, :, 1 - p.y, p.x, 0], y2.at[w], sy2.at[w], ry2.at[w], p.yn)

    def down_copy(u, j):
        return remote(own.at[u, j], zin.at[u, j], szd.at[u, j], rzd.at[u, j], p.below)

    def up_copy(u):
        return remote(own.at[u, 1], zup.at[u], szu.at[u], rzu.at[u], p.above)

    def fin_copy(u, j):
        return remote(own.at[u, j, 1 - p.c], o_fin.at[u], sfin.at[u], rfin.at[u], p.partner)

    def fin_local(u, j):
        return local(own.at[u, j, p.c], o_fin.at[u], lfin.at[u])

    def sent(w):
        x1_copy(w).wait_send()
        y1_copy(w).wait_send()
        x2_copy(w).wait_send()
        y2_copy(w).wait_send()

    def stage_one(u):
        w = lax.rem(u, SLOTS)
        when(u >= SLOTS)(lambda: sent(w))
        load = local(o_grads.at[u], held.at[w], held_sem.at[0])
        load.start()
        load.wait()
        x1_copy(w).start()
        y1_copy(w).start()

    def stage_two(u):
        w = lax.rem(u, SLOTS)
        x1_copy(w).wait_recv()
        held[w, :, 1 - p.y, p.x, 0] += x1[w, :, 1 - p.y]
        held[w, :, p.y, p.x, 0] += x1[w, :, p.y]
        y1_copy(w).wait_recv()
        held[w, :, p.y, 1 - p.x, 1] += y1[w, :, 1 - p.x]
        held[w, :, p.y, p.x, 1] += y1[w, :, p.x]
        y2_copy(w).start()
        x2_copy(w).start()

    def stage_three(u):
        w = lax.rem(u, SLOTS)
        y2_copy(w).wait_recv()
        own[u, :, 0] = held[w, :, p.y, p.x, 0] + y2[w]
        x2_copy(w).wait_recv()
        own[u, :, 1] = held[w, :, p.y, p.x, 1] + x2[w]

        @when(level == 3)
        def _():
            down_copy(u, 0).start()
            down_copy(u, 1).start()

        @when(level == 0)
        def _():
            up_copy(u).start()

    def level_two(u):
        for j in range(2):
            down_copy(u, j).wait_recv()
            own[u, j] += zin[u, j]
            down_copy(u, j).start()

    def level_one(u):
        down_copy(u, 0).wait_recv()
        own[u, 0] += zin[u, 0]
        down_copy(u, 0).start()
        down_copy(u, 1).wait_recv()
        up_copy(u).wait_recv()
        own[u, 1] += zin[u, 1] + zup[u]
        fin_local(u, 1).start()
        fin_copy(u, 1).start()

    def level_zero(u):
        down_copy(u, 0).wait_recv()
        own[u, 0] += zin[u, 0]
        fin_local(u, 0).start()
        fin_copy(u, 0).start()

    def service(s):
        def unit(k, step, extra=True):
            when((k >= 0) & (k < TOTAL) & extra)(lambda: step(k))

        unit(s, stage_one)
        unit(s - 1, stage_two)
        unit(s - 2, stage_three)
        unit(s - 3, level_two, level == 2)
        unit(s - 4, level_one, level == 1)
        unit(s - 5, level_zero, level == 0)
        act_step(s)

    def loads(l):
        whole = (
            (i_c, c_in),
            (i_u, u_in),
            (i_n2, n2),
            (i_m, m_in),
            (i_a, a),
            (i_qk, qk),
            (i_v, v),
            (i_n1, n1),
            (i_h, h_in),
        )
        return [local(src.at[l], dst, load_sem.at[n]) for n, (src, dst) in enumerate(whole)]

    def load_a(l):
        return local(i_wa.at[:, l], wa, unit_sem.at[4])

    def load_m(l, i):
        return local(i_wm.at[:, l, i], wm.at[:, i], unit_sem.at[i])

    def swap(slot):
        copy = remote(part, other.at[slot], swap_sem.at[slot], swap_sem.at[2 + slot], p.partner)
        copy.start()
        copy.wait()

    def put(u, j, value):
        stage[j] = value.reshape(2, 2, 2, 96, BLOCK)
        local(stage.at[j], o_grads.at[u, j], stage_sem.at[j]).start()

    def put_done(u):
        for j in range(2):
            local(stage.at[j], o_grads.at[u, j], stage_sem.at[j]).wait()

    def small_row(l, row, value):
        small[l, row : row + 1] = value[:, :BLOCK]
        small[l, row + 1 : row + 2] = value[:, BLOCK:]

    def norm_back(slot, l, source, gain, first):
        def rows_of(r, carry):
            rows = pl.ds(pl.multiple_of(r * 128, 128), 128)
            upstream = part[rows] + other[slot, rows]
            scaled, inverse = normalize_parts(source[rows])
            lowered, gain_grad, shift_grad = normalize_back(upstream, scaled, inverse, gain)
            value = grad[rows] + lowered
            grad[rows] = value
            rounded = value.astype(bf16)
            low[rows] = rounded
            bias_grad = jnp.sum(rounded.astype(f32), axis=0)
            return (
                carry[0] + gain_grad.reshape(1, WIDTH),
                carry[1] + shift_grad.reshape(1, WIDTH),
                carry[2] + bias_grad.reshape(1, WIDTH),
            )

        zero = jnp.zeros((1, WIDTH), f32)
        sums = lax.fori_loop(0, ROWS // 128, rows_of, (zero, zero, zero))
        small_row(l, first, sums[0])
        small_row(l, first + 2, sums[1])
        return sums[2]

    keep = lax.broadcasted_iota(jnp.int32, (ROWS, ROWS), 1) < FRAMES

    def attention_back(j, carry):
        mixture_back = contract_last(low[...], wa[j, 1, 192:384]).astype(bf16)
        parts = ([], [], [])
        for h in range(HEADS_HERE):
            cols = slice(HEAD_DIM * h, HEAD_DIM * (h + 1))
            k_cols = slice(192 + HEAD_DIM * h, 192 + HEAD_DIM * (h + 1))
            qh, kh, vh, dah = qk[j, :, cols], qk[j, :, k_cols], v[j, :, cols], mixture_back[:, cols]
            scores = jnp.where(keep, contract_last(qh, kh) * score_scale, -1e30)
            weight = jnp.exp(scores - jnp.max(scores, axis=-1, keepdims=True))
            weight = weight * (1.0 / jnp.sum(weight, axis=-1, keepdims=True))
            prob_grad = contract_last(dah, vh)
            centre = jnp.sum(prob_grad * weight, axis=-1, keepdims=True)
            score_back = (weight * (prob_grad - centre)).astype(bf16)
            parts[0].append((product(score_back, kh) * score_scale).astype(bf16))
            parts[1].append((contract_rows(score_back, qh) * score_scale).astype(bf16))
            parts[2].append(contract_rows(weight.astype(bf16), dah).astype(bf16))
        dqk[j] = jnp.concatenate(parts[0] + parts[1], axis=-1)
        dv[j] = jnp.concatenate(parts[2], axis=-1)
        return carry

    local(i_ct, grad, once_sem.at[0]).start()
    small[...] = jnp.zeros_like(small)

    def layer(step, carry):
        l = LAYERS - 1 - step
        u0 = UNITS * step
        s0 = 4 * step
        params = vec[l]
        fetch = loads(l)
        for copy in fetch[:2]:
            copy.start()
        for i in (2, 3, 0, 1):
            load_m(l, i).start()
        for copy in fetch[2:]:
            copy.start()
        load_a(l).start()

        @when(step == 0)
        def _():
            local(i_ct, grad, once_sem.at[0]).wait()
            low[...] = grad[...].astype(bf16)
            small_row(l, 10, jnp.sum(low[...].astype(f32), axis=0, keepdims=True))

        fetch[0].wait()
        for i in (0, 1):
            for j in range(2):
                put(u0 + i, j, contract_rows(low[...], c_in[j, i]))
            put_done(u0 + i)
            if i == 0:
                service(s0)
            else:
                when(step == 0)(lambda: service(1))
        for i in range(2):
            load_m(l, 2 + i).wait()

        @when(step == 0)
        def _():
            for h in range(2):
                for j in range(2):
                    term = contract_last(c_in[j, h], wm[j, 2 + h])
                    if h == 0 and j == 0:
                        part[...] = term
                    else:
                        part[...] += term
            swap(1)
            fetch[3].wait()
            part[...] = m_in[...] + (part[...] + other[1]) + params[5:6]
            keep_top = local(part, o_src.at[0], once_sem.at[1])
            keep_top.start()
            act_local(part, 1, "start")
            keep_top.wait()
            act_local(part, 1, "wait")

        fetch[1].wait()
        fetch[2].wait()
        for i in (2, 3):
            h = i - 2
            load_m(l, h).wait()
            for j in range(2):
                back = (product(low[...], wm[j, 2 + h]) * gelu_slope(u_in[j, h])).astype(bf16)
                row = 14 + 2 * j + h
                small[l, row : row + 1] = jnp.sum(back.astype(f32), axis=0, keepdims=True)
                put(u0 + i, j, contract_rows(n2[...], back))
                term = contract_last(back, wm[j, h])
                if h == 0 and j == 0:
                    part[...] = term
                else:
                    part[...] += term
            put_done(u0 + i)
        service(s0 + 2 - step)
        swap(0)

        @when(step > 0)
        def _():
            fetch[3].wait()

        small_row(l, 8, norm_back(0, l, m_in, params[2:3], 4))

        for copy in fetch[4:]:
            copy.wait()
        load_a(l).wait()
        when(step == 0)(lambda: act_local(h_in, 0, "start"))
        lax.fori_loop(0, 2, attention_back, 0)
        service(s0 + 3 - step)
        for j in range(2):
            stage[j, :, :, :, :, 0:192] = contract_rows(n1[...], dv[j]).reshape(2, 2, 2, 96, 192)
            stage[j, :, :, :, :, 192:384] = contract_rows(low[...], a[j]).reshape(2, 2, 2, 96, 192)
            local(stage.at[j], o_grads.at[u0 + 4, j], stage_sem.at[j]).start()
        put_done(u0 + 4)
        for j in range(2):
            put(u0 + 5, j, contract_rows(n1[...], dqk[j]))
            sums = jnp.sum(dqk[j].astype(f32), axis=0, keepdims=True)
            small[l, 12 + j : 13 + j, 0:192] = sums[:, 0:192]
            small[l, 12 + j : 13 + j, 192:384] = jnp.sum(dv[j].astype(f32), axis=0, keepdims=True)
            term = product(dqk[j], wa[j, 0]) + product(dv[j], wa[j, 1, 0:192])
            if j == 0:
                part[...] = term
            else:
                part[...] += term
        put_done(u0 + 5)
        swap(1)
        down_sum = norm_back(1, l, h_in, params[0:1], 0)

        @when(l > 0)
        def _():
            small_row(l - 1, 10, down_sum)

        when(step == 0)(lambda: act_local(h_in, 0, "wait"))
        return carry

    lax.fori_loop(0, LAYERS, layer, 0)
    keep_grad = local(grad, o_src.at[1], once_sem.at[1])
    keep_grad.start()
    act_local(grad, 2, "start")
    keep_grad.wait()

    def small_copy(m, device):
        return remote(small, small_in.at[m], small_send.at[m], small_recv.at[m], device)

    def small_add(m, device):
        small_copy(m, device).wait()
        small[...] += small_in[m]

    first = STEPS_INSIDE

    def small_step(s):
        @when(s == first)
        def _():
            small_copy(0, p.xn).start()

        @when(s == first + 1)
        def _():
            small_add(0, p.xn)
            small_copy(1, p.yn).start()

        @when(s == first + 2)
        def _():
            small_add(1, p.yn)

            @when((level == 0) | (level == 2))
            def _():
                small_copy(2, p.above).start()

            @when((level == 1) | (level == 3))
            def _():
                small_copy(2, p.below).start()

        @when(s == first + 3)
        def _():
            small_add(2, p.above)

            @when(level == 1)
            def _():
                small_copy(3, p.above).start()

            @when(level == 2)
            def _():
                small_copy(3, p.below).start()

        @when(s == first + 4)
        def _():
            @when((level == 1) | (level == 2))
            def _():
                small_add(3, p.above)

            @when(level == 1)
            def _():
                small_copy(4, p.below).start()

            @when(level == 2)
            def _():
                small_copy(4, p.above).start()

        @when(s == first + 5)
        def _():
            @when((level == 0) | (level == 3))
            def _():
                small_copy(4, p.above).wait_recv()
                small[...] = small_in[4]

            small_copy(5, p.partner).start()
            local(small, o_small.at[0], once_sem.at[2]).start()

        @when(s == first + 6)
        def _():
            small_copy(5, p.partner).wait()
            local(small_in.at[5], o_small.at[1], once_sem.at[3]).start()

            @when((level == 1) | (level == 2))
            def _():
                small_copy(4, p.above).wait_send()

    def step_after(s, carry):
        small_step(s)
        service(s)
        return carry

    lax.fori_loop(first, TOTAL + 5, step_after, 0)

    for w in range(SLOTS):
        sent(w)

    def drain(u, carry):
        @when(level > 0)
        def _():
            down_copy(u, 0).wait_send()

        @when(level > 1)
        def _():
            down_copy(u, 1).wait_send()
            fin_copy(u, 0).wait_recv()

        @when(level == 0)
        def _():
            up_copy(u).wait_send()

        @when(level < 2)
        def _():
            fin_local(u, 0).wait()
            fin_copy(u, 0).wait_send()

        act_drain(u)
        return carry

    assert n_chunks == TOTAL
    lax.fori_loop(0, TOTAL, drain, 0)

    act_local(grad, 2, "wait")
    local(small, o_small.at[0], once_sem.at[2]).wait()
    local(small_in.at[5], o_small.at[1], once_sem.at[3]).wait()


STEPS_INSIDE = 4 + 3
SMALL = (LAYERS, 24, BLOCK)


def run_backward(saved, vectors):
    dma = pltpu.SemaphoreType.DMA
    slots = dma((SLOTS,))
    units = dma((TOTAL,))
    pair = dma((TOTAL, 2))
    return pl.pallas_call(
        backward_kernel,
        out_shape=(
            jax.ShapeDtypeStruct((TOTAL, 96, BLOCK), f32),
            jax.ShapeDtypeStruct((3, 2, ROWS, WIDTH), f32),
            jax.ShapeDtypeStruct((2, *SMALL), f32),
            jax.ShapeDtypeStruct((2, ROWS, WIDTH), f32),
            jax.ShapeDtypeStruct((TOTAL, 2, 2, 2, 2, 96, BLOCK), f32),
        ),
        in_specs=[ANY] * 12 + [VMEM],
        out_specs=(ANY,) * 5,
        scratch_shapes=[
            pltpu.VMEM((SLOTS, 2, 2, 2, 2, 96, BLOCK), f32),
            pltpu.VMEM((SLOTS, 2, 2, 96, BLOCK), f32),
            pltpu.VMEM((SLOTS, 2, 2, 96, BLOCK), f32),
            pltpu.VMEM((SLOTS, 2, 96, BLOCK), f32),
            pltpu.VMEM((SLOTS, 2, 96, BLOCK), f32),
            pltpu.VMEM((TOTAL, 2, 2, 96, BLOCK), f32),
            pltpu.VMEM((TOTAL, 2, 2, 96, BLOCK), f32),
            pltpu.VMEM((TOTAL, 2, 96, BLOCK), f32),
            pltpu.VMEM((2, 2, 2, 2, 96, BLOCK), f32),
            pltpu.VMEM((ROWS, WIDTH), f32),
            pltpu.VMEM((ROWS, WIDTH), f32),
            pltpu.VMEM((2, ROWS, WIDTH), f32),
            pltpu.VMEM((ROWS, WIDTH), f32),
            pltpu.VMEM((ROWS, WIDTH), f32),
            pltpu.VMEM((ROWS, WIDTH), bf16),
            pltpu.VMEM((ROWS, WIDTH), bf16),
            pltpu.VMEM((2, ROWS, BLOCK), bf16),
            pltpu.VMEM((2, ROWS, 192), bf16),
            pltpu.VMEM((2, ROWS, 192), bf16),
            pltpu.VMEM((2, 2, ROWS, BLOCK), f32),
            pltpu.VMEM((2, 2, ROWS, BLOCK), bf16),
            pltpu.VMEM((2, 2, BLOCK, WIDTH), bf16),
            pltpu.VMEM((2, 4, WIDTH, BLOCK), bf16),
            pltpu.VMEM((ROWS, WIDTH), bf16),
            pltpu.VMEM((2, ROWS, BLOCK), bf16),
            pltpu.VMEM((2, ROWS, 192), bf16),
            pltpu.VMEM(SMALL, f32),
            pltpu.VMEM((6, *SMALL), f32),
            slots,
            slots,
            slots,
            slots,
            slots,
            slots,
            slots,
            slots,
            pair,
            pair,
            units,
            units,
            units,
            units,
            units,
            dma((TOTAL, 3)),
            dma((TOTAL, 2)),
            dma((3,)),
            dma((9,)),
            dma((5,)),
            dma((2,)),
            dma((1,)),
            dma((4,)),
            dma((6,)),
            dma((6,)),
            dma((4,)),
        ],
        compiler_params=pltpu.CompilerParams(
            collective_id=1, has_side_effects=True, vmem_limit_bytes=63 << 20
        ),
        name="backward_reduce",
    )(*saved, vectors)


def per_device(
    frames,
    cotangent,
    w_attn,
    w_mlp,
    vectors,
    head_bias,
    up_bias,
    moment_attn,
    square_attn,
    moment_mlp,
    square_mlp,
    moment_vectors,
    square_vectors,
    moment_head,
    square_head,
    moment_up,
    square_up,
):
    dp = lax.axis_index("dp")
    t = lax.axis_index("tensor")
    core = dp % 2
    dp_size = lax.axis_size("dp")

    wa = jnp.swapaxes(w_attn, 2, 3).reshape(LAYERS, 4, 4, 2, 24, WIDTH)
    wm = w_mlp.reshape(LAYERS, 2, 4, 2, 96, 2 * BLOCK)
    saved = run_forward(frames, cotangent, wa, wm, head_bias, up_bias, vectors)
    fin, acts, small, _, _ = run_backward(saved, vectors)
    sections = jnp.concatenate([acts[:2, 0, :FRAMES], acts[:2, 1, :FRAMES]], axis=1)
    upstream = jnp.concatenate([acts[2, 0, :FRAMES], acts[2, 1, :FRAMES]], axis=0)

    if dp_size > GROUP:
        groups = [[i + GROUP * o for o in range(dp_size // GROUP)] for i in range(GROUP)]
        small = lax.psum(small, "dp", axis_index_groups=groups)
    vector_all = small[0, :, :12].reshape(LAYERS, 6, WIDTH)
    owner = t // 2
    here = jnp.where(owner == core, small[0], small[1])
    second = jnp.where(owner == 0, t % 2, 1 - t % 2)
    head_all = jnp.where(second == 0, here[:, 12], here[:, 13]).reshape(LAYERS, 2, HEADS_HERE, HEAD_DIM)
    up_all = jnp.where(second == 0, here[:, 14:16], here[:, 16:18]).reshape(LAYERS, 12, HEAD_DIM)

    def owned(param, dim):
        size = param.shape[dim] // dp_size
        return lax.dynamic_slice_in_dim(param, dp * size, size, dim)

    if dp_size > GROUP:
        rows = jnp.zeros((TOTAL, WIDTH, BLOCK), f32)
        rows = lax.dynamic_update_slice_in_dim(rows, fin, (dp % GROUP) * 96, 1)
        fin = lax.psum_scatter(rows, "dp", scatter_dimension=1, tiled=True)

    def unit(l, k):
        return fin[(LAYERS - 1 - l) * UNITS + k]

    attn_grad = jnp.stack(
        [
            jnp.stack([unit(l, 5)[:, :192], unit(l, 5)[:, 192:], unit(l, 4)[:, :192], unit(l, 4)[:, 192:]])
            for l in range(LAYERS)
        ]
    )
    mlp_grad = jnp.stack(
        [
            jnp.stack(
                [
                    jnp.concatenate([unit(l, 2), unit(l, 3)], axis=-1),
                    jnp.concatenate([unit(l, 0), unit(l, 1)], axis=-1),
                ]
            )
            for l in range(LAYERS)
        ]
    )
    attn = adamw_update(owned(w_attn, 2), attn_grad, moment_attn, square_attn, rate_matrix)
    mlp = adamw_update(owned(w_mlp, 2), mlp_grad, moment_mlp, square_mlp, rate_matrix)
    vector_new = adamw_update(
        owned(vectors, 2), owned(vector_all, 2), moment_vectors, square_vectors, rate_vector
    )
    head = adamw_update(owned(head_bias, 3), owned(head_all, 3), moment_head, square_head, rate_vector)
    upper = adamw_update(owned(up_bias, 2), owned(up_all, 2), moment_up, square_up, rate_vector)
    return (sections, upstream, *attn, *mlp, *vector_new, *head, *upper)


def solution(mesh):
    in_specs = (
        P("dp", None),
        P("dp", None),
        P(None, None, None, "tensor"),
        P(None, None, None, "tensor"),
        P(),
        P(None, None, "tensor", None),
        P(None, "tensor", None),
        P(None, None, "dp", "tensor"),
        P(None, None, "dp", "tensor"),
        P(None, None, "dp", "tensor"),
        P(None, None, "dp", "tensor"),
        P(None, None, "dp"),
        P(None, None, "dp"),
        P(None, None, "tensor", "dp"),
        P(None, None, "tensor", "dp"),
        P(None, "tensor", "dp"),
        P(None, "tensor", "dp"),
    )
    out_specs = (
        P(None, "dp", None),
        P("dp", None),
        P(None, None, "dp", "tensor"),
        P(None, None, "dp", "tensor"),
        P(None, None, "dp", "tensor"),
        P(None, None, "dp", "tensor"),
        P(None, None, "dp", "tensor"),
        P(None, None, "dp", "tensor"),
        P(None, None, "dp"),
        P(None, None, "dp"),
        P(None, None, "dp"),
        P(None, None, "tensor", "dp"),
        P(None, None, "tensor", "dp"),
        P(None, None, "tensor", "dp"),
        P(None, "tensor", "dp"),
        P(None, "tensor", "dp"),
        P(None, "tensor", "dp"),
    )
    return jax.shard_map(
        per_device, mesh=mesh, in_specs=in_specs, out_specs=out_specs, check_vma=False
    )
```

time: 649 us -> 515 us (0.79); the launches traced: 639 us -> 515 us
  Pallas kernels: 570 us -> 482 us
  local copies, waits for them, and re-layouts: 41.2 us -> 17.7 us
  other arithmetic: 26 us -> 13.7 us
    pallas_call x1, Pallas kernels: 355 us -> 294 us  [run_backward(): pl.pallas_call(backward_kernel, out_shape=(jax.ShapeDtypeStruct((TOTAL, 9...]
    pallas_call x1, Pallas kernels: 216 us -> 188 us  [run_forward(): pl.pallas_call(forward_kernel, out_shape=(hbm((ROWS, WIDTH), f32), hbm((L...]
    slice x6 -> x0, local copies, waits for them, and re-layouts: 20.1 us -> none  [the longest x1 7.84 us: per_device(): acts = acts[:, :, :FRAMES]]
    select_n x1 -> x0, other arithmetic: 7.61 us -> none  [per_device(): acts = jnp.where(core == 0, acts, acts[::-1])]
where the time goes in v3:
time: 515 us
  Pallas kernels  482 us (94%)
  local copies, waits for them, and re-layouts  17.7 us (3%)
  other arithmetic  13.7 us (3%)
    pallas_call x1, Pallas kernels, run_backward(): pl.pallas_call(backward_kernel, out_shape=(jax.ShapeDtypeStruct((TOTAL, 9...  294 us
    pallas_call x1, Pallas kernels, run_forward(): pl.pallas_call(forward_kernel, out_shape=(hbm((ROWS, WIDTH), f32), hbm((L...  188 us
    unnamed x48, local copies, waits for them, and re-layouts  10.4 us

profile of v3, /device:TPU:0, one launch (start us, length us, event | category | flops | bytes accessed | tf_op | source)
XLA Modules:
  0.0 514.6 jit_solution(14421550948358395093)
XLA Ops:
  0.7 1.4 copy.70.vec
  2.0 1.3 copy.68.head_bias
  3.3 1.3 copy.69.up_bias
  4.6 188.2 %gather_forward.1 = (f32[512,768]{1,0:T(8,128)}, f32[2,512,768]{2,1,0:T(8,128)}, f32[2,512,768]{2,1,0:T(8,128)}, bf16[2,512,768]{2,1,0:T(8,128)(2,1)}, bf16[2,51...) custom-call(f32[1000,768]{1,0:T(8,128)} %frames.1, ...), custom_call_target="tpu_custom_call" | custom-call | tf_op jit(solution)/shard_map/gather_forward/pallas_call | solution.py:639
  192.9 294.0 %backward_reduce.1 = (f32[12,96,384]{2,1,0:T(8,128)}, f32[3,2,512,768]{3,2,1,0:T(8,128)}, f32[2,2,24,384]{3,2,1,0:T(8,128)}, f32[2,512,768]{2,1,0:T(8,128)}, f32[12,2,2,2,2,96,384]{6,5,4,3,2,1,0:T(8,128)}) custom-call(f32[512,768]{1,0:T(8,128)} %get-tuple-element.32.i_ct, f32[2,512,768]{2,1,0:T(8,128)} %get-tuple-element.33.i_h, ...), custom_call_target="tpu_custom_call" | custom-call | tf_op jit(solution)/shard_map/backward_reduce/pallas_call | solution.py:1279
  486.9 2.4 slice_bitcast_fusion.11
  489.5 1.1 copy-done
  490.6 0.4 copy-done.1
  490.9 3.7 multiply_subtract_fusion
  494.8 0.7 copy-done.2
  495.7 1.7 constant_dynamic-slice_fusion.2
  497.4 0.3 copy.88
  497.8 3.3 multiply_subtract_fusion.1
  501.1 2.2 slice_bitcast_fusion.3
  503.3 1.9 pad_maximum_fusion.1
  505.7 3.1 pad_maximum_fusion
  509.2 0.6 multiply_subtract_fusion.2
  510.1 0.6 copy.85
  510.7 0.6 copy.86
  511.3 0.6 copy.87
  511.9 0.8 multiply_subtract_fusion.4
  512.8 0.6 copy.82
  513.4 0.6 copy.83
  514.0 0.6 copy.84
  (56 shorter events, 1.6 us)
Async XLA Ops:
  489.3 1.3 copy-start
  489.3 1.6 copy-start.1
  490.9 3.7 copy-start.4
  490.9 3.7 copy-start.5
  494.6 0.9 copy-start.2
  494.6 1.0 copy-start.3
  497.4 7.7 %slice-start = ((s8[9437184]{0:T(1024)(128)(4,1)}), s8[1048576]{0:T(1024)(128)(4,1)S(1)}, s32[]{:S(2)}) async-start(s8[9437184]{0:T(1024)(128)(4,1)} %bitcast.71), calls=%async_computation | async-start | bytes 2097152
  497.8 7.4 %slice-start.1 = ((s8[9437184]{0:T(1024)(128)(4,1)}), s8[4194304]{0:T(1024)(128)(4,1)S(1)}, s32[]{:S(2)}) async-start(s8[9437184]{0:T(1024)(128)(4,1)} %bitcast.71), calls=%async_computation.1 | async-start | bytes 8388608
  501.1 4.1 slice-start.2
  505.6 3.2 copy-start.6
  505.6 3.5 copy-start.8
  505.6 3.6 copy-start.9
  505.6 3.6 copy-start.10
  505.6 4.4 copy-start.7
  505.6 4.4 copy-start.11
  505.6 4.4 copy-start.12
  505.7 6.3 %copy-start.13 = (f32[2,6,96]{2,0,1:T(2,128)S(1)}, f32[2,6,96]{2,0,1:T(2,128)}, u32[]{:S(2)}) copy-start(f32[2,6,96]{2,0,1:T(2,128)} %param.28) | copy-start | bytes 13828
  505.7 6.3 %copy-start.14 = (f32[2,6,96]{2,0,1:T(2,128)S(1)}, f32[2,6,96]{2,0,1:T(2,128)}, u32[]{:S(2)}) copy-start(f32[2,6,96]{2,0,1:T(2,128)} %param.29) | copy-start | bytes 13828
